TPU v7x, 32 devices: a whole 2x2x4 slice. The times are simulated.
32 devices in a mesh: ctx: 8 (over y, x, core), exp: 4 (over z).
Axes of the slice: x: 2, y: 2, z: 4, core: 2. Of those that a mesh axis runs over, the one named last changes fastest.
Arguments:
- residual: bfloat16 [1536, 2048], P('ctx', 'exp'), may hold values from -40 to 40
- queries: bfloat16 [1536, 2048], P('ctx', 'exp'), may hold values from -32 to 32
- keys: bfloat16 [1536, 2048], P('ctx', 'exp'), may hold values from -8 to 8
- values: bfloat16 [1536, 2048], P('ctx', 'exp'), may hold values from -6 to 6
- w_out: bfloat16 [2048, 2048], P('exp'), may hold values from -0.1875 to 0.1875
- moe_gain: float32 [2048], replicated, may hold values from 0.1 to 1.9
- expert_ids: int32 [1536, 8], P('ctx'), may hold values from 0 to 63, all different within a row; in each aligned block of 192 rows (0 to 191, 192 to 383, ...) at most 36 rows name the same one
- gate_weights: float32 [1536, 8], P('ctx'), may hold values from 0.05 to 0.5
- w_gate: bfloat16 [64, 2048, 1024], P('ctx', None, 'exp'), may hold values from -1 to 1
- w_up: bfloat16 [64, 2048, 1024], P('ctx', None, 'exp'), may hold values from -1 to 1
- w_down: bfloat16 [64, 1024, 2048], P('ctx', None, 'exp'), may hold values from -0.01171875 to 0.01171875
Outputs:
- mixed: bfloat16 [1536, 2048], P('ctx', 'exp')
Inputs may be any that keep to these rules, and one draw needn't show every extreme that they name: `expert_ids`: each row names 8 different experts. Within the 192 rows of one block (rows b * 192 to b * 192 + 191) no expert is named more than 36 times, and in every draw some expert is named exactly 36 times in some block.
All inputs are finite; a program needn't handle non-finite values.
Results may differ from a plain program's by a relative error of at most 0.015.
Values may be sent and summed in bfloat16 or wider, within the bound.
A program may use at most 128 MiB of HBM per device.

v0:
```python
import math

import jax
import jax.numpy as jnp
from jax import lax
from jax.sharding import PartitionSpec as P

D = 2048
H = 16
K = 8
CAP = 36


epsilon = 1e-05


def attend(carried, pieces, q_three, query_pos):
    row_max, row_total, row_accum = carried
    key_piece, value_piece = pieces
    piece_rows = key_piece.shape[0]
    heads_here = q_three.shape[1]
    head_dim = q_three.shape[2]
    k_three = key_piece.reshape(piece_rows, heads_here, head_dim)
    v_three = value_piece.reshape(piece_rows, heads_here, head_dim)
    score_scale = 1.0 / math.sqrt(head_dim)
    scores = (
        jnp.einsum("qhd,khd->qhk", q_three, k_three, preferred_element_type=jnp.float32)
        * score_scale
    )
    allowed = (jnp.arange(piece_rows, dtype=jnp.int32)[None, :] <= query_pos[:, None])[:, None, :]
    masked = jnp.where(allowed, scores, -1e30)
    new_max = jnp.maximum(row_max, jnp.max(masked, axis=2))
    weights = jnp.where(allowed, jnp.exp(masked - new_max[:, :, None]), 0.0)
    row_total = jnp.sum(weights, axis=2)
    update = jnp.einsum(
        "qhk,khd->qhd", weights.astype(jnp.bfloat16), v_three, preferred_element_type=jnp.float32
    )
    row_accum = update
    return (new_max, row_total, row_accum)


def local(
    residual, queries, keys, values, w_out, moe_gain, expert_ids, gate_weights, w_gate, w_up, w_down
):
    block_rows, col_width = queries.shape
    head_dim = D // H
    heads_here = col_width // head_dim
    experts_here = w_gate.shape[0]
    units_here = w_gate.shape[2]
    columns = lax.axis_size("ctx")
    experts_all = experts_here * columns
    ctx_index = lax.axis_index("ctx")
    exp_index = lax.axis_index("exp")
    query_pos = ctx_index * block_rows + jnp.arange(block_rows, dtype=jnp.int32)
    q_three = queries.reshape(block_rows, heads_here, head_dim)
    start_state = (
        jnp.full((block_rows, heads_here), -1e30, jnp.float32),
        jnp.zeros((block_rows, heads_here), jnp.float32),
        jnp.zeros((block_rows, heads_here, head_dim), jnp.float32),
    )
    row_max, row_total, row_accum = attend(
        start_state,
        (
            lax.all_gather(keys, "ctx", axis=0, tiled=True),
            lax.all_gather(values, "ctx", axis=0, tiled=True),
        ),
        q_three,
        query_pos,
    )
    attn_heads = (
        (row_accum / row_total[:, :, None]).reshape(block_rows, col_width).astype(jnp.bfloat16)
    )
    flat_ids = expert_ids.reshape(-1)
    onehot = (flat_ids[:, None] == jnp.arange(experts_all, dtype=jnp.int32)[None, :]).astype(
        jnp.int32
    )
    rank_in = jnp.cumsum(onehot, axis=0) - 1
    slot_of = jnp.sum(rank_in * onehot, axis=1)
    token_of = jnp.arange(block_rows * K, dtype=jnp.int32) // K
    slot_table = jnp.full((experts_all, CAP), -1, jnp.int32).at[flat_ids, slot_of].set(token_of)
    is_filled = (slot_table >= 0)[:, :, None]
    safe_index = jnp.maximum(slot_table, 0)
    w_in = jnp.concatenate([w_gate, w_up], axis=2)
    attn_cols = (
        lax.psum_scatter(
            jnp.einsum("tf,fc->ct", attn_heads, w_out, preferred_element_type=jnp.float32).astype(
                jnp.bfloat16
            ),
            "exp",
            scatter_dimension=0,
            tiled=True,
        )
        .astype(jnp.float32)
        .T
    )
    post_cols = (residual.astype(jnp.float32) + attn_cols).astype(jnp.bfloat16)
    cols_wide = post_cols.astype(jnp.float32)
    square_sum = lax.psum(jnp.sum(cols_wide * cols_wide, axis=1), "exp")
    gain_cols = lax.dynamic_slice_in_dim(moe_gain, exp_index * col_width, col_width)
    moe_cols = (cols_wide * lax.rsqrt(square_sum / D + epsilon)[:, None] * gain_cols).astype(
        jnp.bfloat16
    )
    packed = jnp.where(is_filled, moe_cols[safe_index], jnp.zeros((), jnp.bfloat16))
    received = lax.all_to_all(
        packed.reshape(columns, experts_here, CAP, moe_cols.shape[1]),
        "ctx",
        split_axis=0,
        concat_axis=0,
        tiled=True,
    )
    w_rows = w_in
    pre_act = jnp.einsum(
        "sjcd,jdf->sjcf",
        lax.all_gather(received, "exp", axis=3, tiled=True),
        w_rows,
        preferred_element_type=jnp.float32,
    )
    hidden = (jax.nn.silu(pre_act[..., :units_here]) * pre_act[..., units_here:]).astype(
        jnp.bfloat16
    )
    w_rows = w_down
    expert_out = jnp.einsum(
        "sjcf,jfd->sjcd",
        lax.all_gather(hidden, "exp", axis=3, tiled=True),
        w_rows,
        preferred_element_type=jnp.float32,
    ).astype(jnp.bfloat16)
    returned = lax.all_to_all(expert_out, "ctx", split_axis=0, concat_axis=0, tiled=True)
    flat_out = returned.reshape(experts_all * CAP, col_width)
    picked = flat_out[flat_ids * CAP + slot_of].reshape(block_rows, K, col_width)
    combined = jnp.einsum("tk,tkd->td", gate_weights, picked.astype(jnp.float32))
    return (post_cols.astype(jnp.float32) + combined).astype(jnp.bfloat16)


def solution(mesh):
    placed = (
        P("ctx", "exp"),
        P("ctx", "exp"),
        P("ctx", "exp"),
        P("ctx", "exp"),
        P("exp", None),
        P(),
        P("ctx", None),
        P("ctx", None),
        P("ctx", None, "exp"),
        P("ctx", None, "exp"),
        P("ctx", None, "exp"),
    )
    return jax.shard_map(
        local, mesh=mesh, in_specs=placed, out_specs=P("ctx", "exp"), check_vma=False
    )
```

profile of v0, /device:TPU:0, one launch (start us, length us, event | category | flops | bytes accessed | tf_op | source)
XLA Modules:
  0.0 519.5 jit_solution(16654188542422320673)
XLA Ops:
  9.2 18.1 %reduce-window.6 = s32[64,12,128]{2,1,0:T(8,128)S(1)} reduce-window(s32[64,12,128]{2,1,0:T(8,128)S(1)} %fusion.30, s32[]{:T(128)} %constant.56.clone.1), window={size=1x1x128 pad=0_0x0_0x127_0}, to_apply=%region_3.4 | reduce-window | flops 12484608 | bytes 786436 | tf_op jit(solution)/shard_map/reduce-window
  28.2 9.5 %all-gather.5.cloned.1.call-done = bf16[1536,512]{1,0:T(8,128)(2,1)} async-done(((bf16[192,512]{1,0:T(8,128)(2,1)}), bf16[1536,512]{1,0:T(8,128)(2,1)}) %all-gather.5.cloned.1.call-update) | async-done | bytes 1572880 | tf_op jit(solution)/shard_map/all_gather | solution.py:64
  37.7 2.6 copy.43
  40.3 2.5 fusion.5
  46.5 18.9 %all-gather.7.cloned.1.call-done = bf16[1536,512]{1,0:T(8,128)(2,1)} async-done(((bf16[192,512]{1,0:T(8,128)(2,1)}), bf16[1536,512]{1,0:T(8,128)(2,1)}) %all-gather.7.cloned.1.call-update) | async-done | bytes 1572880 | tf_op jit(solution)/shard_map/all_gather | solution.py:65
  65.3 2.6 copy.46
  67.9 4.2 fusion.27
  74.3 6.2 %scatter_custom_fusion = s32[2304]{0:T(1024)S(1)} fusion(s32[1536]{0:T(1024)S(1)} %get-tuple-element.11, s32[1536]{0:T(1024)S(1)} %get-tuple-element.10, s32[]{:T(128)} %constant.30.clone.1), kind=kCustom, calls=%fused_computation.69 | custom fusion | bytes 9220
  81.8 15.3 %reduce-scatter.2.cloned.1.call-done = bf16[512,192]{0,1:T(8,128)(2,1)} async-done(((bf16[2048,192]{0,1:T(8,128)(2,1)}), bf16[512,192]{0,1:T(8,128)(2,1)}) %reduce-scatter.2.cloned.1.call-update) | async-done | bytes 196624 | tf_op jit(solution)/shard_map/reduce_scatter | solution.py:85
  98.2 10.0 %psum.7 = f32[192]{0:T(256)S(1)} all-reduce(f32[192]{0:T(256)S(1)} %fusion.31), channel_id=1, replica_groups=mesh['ctx'=8,'exp'=4] {'exp'}, use_global_device_ids=true, to_apply=%region_8.9 | all-reduce | flops 192 | bytes 1536 | tf_op jit(solution)/shard_map/psum | solution.py:98
  109.3 7.5 %gather_fusion = bf16[2304,512]{1,0:T(8,128)(2,1)} fusion(bf16[192,512]{1,0:T(8,128)(2,1)S(1)} %fusion.33, s32[3072]{0:T(1024)S(1)} %pad_clamp_fusion), kind=kCustom, calls=%fused_computation | custom fusion | bytes 4727808 | tf_op jit(solution)/shard_map/gather | solution.py:103
  116.8 4.7 gather.9
  124.3 32.9 %all_to_all.10 = bf16[8,8,36,512]{3,1,2,0:T(8,128)(2,1)S(1)} all-to-all(bf16[8,8,36,512]{3,1,2,0:T(8,128)(2,1)S(1)} %copy.56), channel_id=1, replica_groups=mesh['ctx'=8,'exp'=4] {'ctx'}, dimensions={0} | all-to-all | bytes 4718592 | tf_op jit(solution)/shard_map/all_to_all | solution.py:104
  157.2 2.4 copy.57
  159.8 180.2 %all-gather.9.cloned.1.call-done = bf16[8,8,36,2048]{3,2,0,1:T(8,128)(2,1)} async-done(((bf16[8,8,36,512]{3,2,0,1:T(8,128)(2,1)}), bf16[8,8,36,2048]{3,2,0,1:T(8,128)(2,1)}) %all-gather.9.cloned.1.call-update) | async-done | bytes 9437200 | tf_op jit(solution)/shard_map/all_gather | solution.py:114
  340.0 11.2 %fusion.9 = f32[8,8,36,512]{3,2,0,1:T(8,128)S(1)} fusion(bf16[8,8,36,2048]{3,2,0,1:T(8,128)(2,1)} %all-gather.9.cloned.1.call-done, bf16[8,2048,256]{2,1,0:T(8,128)(2,1)} %param.20, bf16[8,2048,256]{2,1,0:T(8,128)(2,1)} %param.19), kind=kOutput, calls=%fused_computation.19 | convolution fusion | flops 4865392640 | bytes 30932992 | tf_op jit(solution)/shard_map/sjcd,jdf->sjcf/dot_general | solution.py:112
  353.2 96.0 %all-gather.11.cloned.1.call-done = bf16[8,8,36,1024]{3,2,0,1:T(8,128)(2,1)} async-done(((bf16[8,8,36,256]{3,2,0,1:T(8,128)(2,1)}), bf16[8,8,36,1024]{3,2,0,1:T(8,128)(2,1)}) %all-gather.11.cloned.1.call-update) | async-done | bytes 4718608 | tf_op jit(solution)/shard_map/all_gather | solution.py:124
  449.3 7.8 %convert_bitcast_fusion = bf16[8,8,36,512]{3,2,0,1:T(8,128)(2,1)S(1)} fusion(bf16[8,8,36,1024]{3,2,0,1:T(8,128)(2,1)} %all-gather.11.cloned.1.call-done, bf16[8,1024,512]{2,1,0:T(8,128)(2,1)} %param.21), kind=kOutput, calls=%fused_computation.16 | convolution fusion | flops 2417098752 | bytes 15466496 | tf_op jit(solution)/shard_map/sjcf,jfd->sjcd/dot_general | solution.py:122
  457.1 2.7 copy.58
  459.8 4.5 all-to-all-start.1
  464.5 29.3 %all-to-all-done.1 = bf16[8,8,36,512]{3,1,2,0:T(8,128)(2,1)} async-done(((bf16[8,8,36,512]{3,1,2,0:T(8,128)(2,1)}), bf16[8,8,36,512]{3,1,2,0:T(8,128)(2,1)}, u32[]{:S(2)}, u32[]{:S(2)}) %all-to-all-start.1) | async-done | bytes 2359328 | tf_op jit(solution)/shard_map/all_to_all | solution.py:128
  493.8 4.1 copy.59
  497.9 4.7 reshape.143
  502.6 7.6 %gather_fusion.1 = bf16[1536,512]{1,0:T(8,128)(2,1)} fusion(bf16[2304,512]{1,0:T(8,128)(2,1)} %reshape.143, s32[2048]{0:T(1024)S(1)} %pad_clamp_fusion.1), kind=kCustom, calls=%fused_computation.1 | custom fusion | bytes 3151872 | tf_op jit(solution)/shard_map/gather | solution.py:130
  (67 shorter events, 20.5 us)
Async XLA Ops:
  6.5 65.6 %copy-start = (bf16[512,2048]{1,0:T(8,128)(2,1)S(1)}, bf16[512,2048]{1,0:T(8,128)(2,1)}, u32[]{:S(2)}) copy-start(bf16[512,2048]{1,0:T(8,128)(2,1)} %param.15) | copy-start | bytes 6291460
  6.5 31.2 %all-gather.5.cloned.1.call-start = ((), (), s32[]{:S(2)}) async-start(), calls=%async_computation.3 | async-start | bytes 1769472 | tf_op jit(solution)/shard_map/all_gather | solution.py:64
  7.3 58.1 %all-gather.7.cloned.1.call-start = ((), (), s32[]{:S(2)}) async-start(), calls=%async_computation.4 | async-start | bytes 1769472 | tf_op jit(solution)/shard_map/all_gather | solution.py:65
  8.0 89.1 %reduce-scatter.2.cloned.1.call-start = ((), (), s32[]{:S(2)}) async-start(), calls=%async_computation.5 | async-start | bytes 983040 | tf_op jit(solution)/shard_map/reduce_scatter | solution.py:85
  27.4 12.9 %copy-start.5 = (bf16[192,512]{1,0:T(8,128)(2,1)S(1)}, bf16[192,512]{1,0:T(8,128)(2,1)}, u32[]{:S(2)}) copy-start(bf16[192,512]{1,0:T(8,128)(2,1)} %param.12) | copy-start | bytes 589828
  42.8 2.1 copy-start.2
  72.1 2.0 copy-start.8
  72.1 2.1 copy-start.7
  72.1 25.0 %copy-start.3 = (bf16[192,512]{1,0:T(8,128)(2,1)S(1)}, bf16[192,512]{1,0:T(8,128)(2,1)}, u32[]{:S(2)}) copy-start(bf16[192,512]{1,0:T(8,128)(2,1)} %param.11) | copy-start | bytes 589828
  73.7 266.3 %all-gather.9.cloned.1.call-start = ((), (), s32[]{:S(2)}) async-start(), calls=%async_computation.6 | async-start | bytes 13107200 | tf_op jit(solution)/shard_map/all_gather | solution.py:114
  159.6 289.7 %all-gather.11.cloned.1.call-start = ((), (), s32[]{:S(2)}) async-start(), calls=%async_computation.7 | async-start | bytes 6553600 | tf_op jit(solution)/shard_map/all_gather | solution.py:124
  459.8 4.5 copy-start.6
  459.8 34.0 %all-to-all-start.1 = ((bf16[8,8,36,512]{3,1,2,0:T(8,128)(2,1)}), bf16[8,8,36,512]{3,1,2,0:T(8,128)(2,1)}, u32[]{:S(2)}, u32[]{:S(2)}) async-start(bf16[8,8,36,512]{3,1,2,0:T(8,128)(2,1)} %copy.58), calls=%async_computation.2 | async-start | bytes 4718592 | tf_op jit(solution)/shard_map/all_to_all | solution.py:128
  502.6 9.6 %copy-start.4 = (bf16[512,192]{0,1:T(8,128)(2,1)S(1)}, bf16[512,192]{0,1:T(8,128)(2,1)}, u32[]{:S(2)}) copy-start(bf16[512,192]{0,1:T(8,128)(2,1)} %reduce-scatter.2.cloned.1.call-done) | copy-start | bytes 589828
  502.6 10.4 %copy-start.1 = (bf16[512,2048]{1,0:T(8,128)(2,1)S(1)}, bf16[512,2048]{1,0:T(8,128)(2,1)}, u32[]{:S(2)}) copy-start(bf16[512,2048]{1,0:T(8,128)(2,1)} %param.15) | copy-start | bytes 6291460
Sparse Core Ops, SparseCore 0:
  9.2 28.4 all-gather.4
  39.6 25.6 all-gather.6
  73.8 23.2 reduce-scatter.1
  159.7 180.2 all-gather.8
  353.3 95.8 all-gather.10
where the time goes:
time: 520 us; the launch traced here: 519 us
  waiting for transfers between devices  351 us (68%)
  local copies, waits for them, and re-layouts  51.1 us (10%)
  blocking collectives  42.9 us (8%)
  matrix products  29.2 us (6%)
  other arithmetic  27.3 us (5%)
  between operations  13.4 us (3%)
    all_gather x1, waiting for transfers between devices, local(): lax.all_gather(received, 'exp', axis=3, tiled=True)  180 us
    all_gather x1, waiting for transfers between devices, local(): lax.all_gather(hidden, 'exp', axis=3, tiled=True)  96 us
    all_to_all x1, blocking collectives, local(): lax.all_to_all(packed.reshape(columns, experts_here, CAP, moe_cols.shape[...  32.9 us
    all_to_all x1, waiting for transfers between devices, local(): lax.all_to_all(expert_out, 'ctx', split_axis=0, concat_axis=0, tiled=True)  29.3 us
    all_gather x1, waiting for transfers between devices, local(): lax.all_gather(values, 'ctx', axis=0, tiled=True)  18.9 us
    another operation x2, other arithmetic  18.2 us
    reduce_scatter x1, waiting for transfers between devices, local(): lax.psum_scatter(jnp.einsum('tf,fc->ct', attn_heads, w_out, preferred_ele...  15.3 us
    gather x2, local copies, waits for them, and re-layouts, local(): moe_cols[safe_index]  12.2 us
  transfers between devices with their start and end apart: 6, of which 6 were waited for; matrix products, arithmetic and copies ran while one was open for 7% of the time, Pallas kernels for 0%

commit v1 on v0

v1 whole, which is shorter than its diff:
```python
import math

import jax
import jax.numpy as jnp
from jax import lax
from jax.sharding import PartitionSpec as P

D = 2048
H = 16
K = 8
CAP = 36
GROUP = 4


epsilon = 1e-05


def attend(carried, pieces, q_three, query_pos):
    row_max, row_total, row_accum = carried
    key_piece, value_piece = pieces
    piece_rows = key_piece.shape[0]
    heads_here = q_three.shape[1]
    head_dim = q_three.shape[2]
    k_three = key_piece.reshape(piece_rows, heads_here, head_dim)
    v_three = value_piece.reshape(piece_rows, heads_here, head_dim)
    score_scale = 1.0 / math.sqrt(head_dim)
    scores = (
        jnp.einsum("qhd,khd->qhk", q_three, k_three, preferred_element_type=jnp.float32)
        * score_scale
    )
    allowed = (jnp.arange(piece_rows, dtype=jnp.int32)[None, :] <= query_pos[:, None])[:, None, :]
    masked = jnp.where(allowed, scores, -1e30)
    new_max = jnp.maximum(row_max, jnp.max(masked, axis=2))
    weights = jnp.where(allowed, jnp.exp(masked - new_max[:, :, None]), 0.0)
    row_total = jnp.sum(weights, axis=2)
    update = jnp.einsum(
        "qhk,khd->qhd", weights.astype(jnp.bfloat16), v_three, preferred_element_type=jnp.float32
    )
    row_accum = update
    return (new_max, row_total, row_accum)


def local(
    residual, queries, keys, values, w_out, moe_gain, expert_ids, gate_weights, w_gate, w_up, w_down
):
    block_rows, col_width = queries.shape
    head_dim = D // H
    heads_here = col_width // head_dim
    experts_here = w_gate.shape[0]
    columns = lax.axis_size("ctx")
    ctx_index = lax.axis_index("ctx")
    query_pos = ctx_index * block_rows + jnp.arange(block_rows, dtype=jnp.int32)
    q_three = queries.reshape(block_rows, heads_here, head_dim)
    start_state = (
        jnp.full((block_rows, heads_here), -1e30, jnp.float32),
        jnp.zeros((block_rows, heads_here), jnp.float32),
        jnp.zeros((block_rows, heads_here, head_dim), jnp.float32),
    )
    row_max, row_total, row_accum = attend(
        start_state,
        (
            lax.all_gather(keys, "ctx", axis=0, tiled=True),
            lax.all_gather(values, "ctx", axis=0, tiled=True),
        ),
        q_three,
        query_pos,
    )
    attn_heads = (
        (row_accum / row_total[:, :, None]).reshape(block_rows, col_width).astype(jnp.bfloat16)
    )
    routing = lax.all_gather(
        jnp.concatenate([expert_ids.astype(jnp.float32), gate_weights], axis=1),
        "ctx",
        axis=0,
        tiled=True,
    )
    here = (ctx_index * experts_here + jnp.arange(experts_here, dtype=jnp.int32)).astype(
        jnp.float32
    )
    match = routing[:, :K, None] == here[None, None, :]
    chosen = jnp.any(match, axis=1)
    gates = jnp.sum(jnp.where(match, routing[:, K:, None], 0.0), axis=1)
    before = jnp.tril(jnp.ones((block_rows, block_rows), jnp.bfloat16), -1)
    rank = jnp.einsum(
        "ut,btj->buj",
        before,
        chosen.astype(jnp.bfloat16).reshape(columns, block_rows, experts_here),
        preferred_element_type=jnp.float32,
    )
    groups = columns // GROUP
    offset = ((jnp.arange(columns) % GROUP) * CAP).astype(jnp.float32)[:, None, None]
    place = jnp.where(
        chosen.reshape(columns, block_rows, experts_here), rank + offset, -1.0
    ).reshape(groups, GROUP * block_rows, experts_here)
    slots = jnp.arange(GROUP * CAP, dtype=jnp.int32).astype(jnp.float32)
    place_t = place.transpose(0, 2, 1)
    pick = place_t[:, :, None, :] == slots[None, None, :, None]
    gates_t = gates.reshape(groups, GROUP * block_rows, experts_here).transpose(0, 2, 1)
    slot_gate = jnp.sum(jnp.where(pick, gates_t[:, :, None, :], 0.0), axis=3)
    pick = pick.astype(jnp.bfloat16)
    attn_cols = lax.psum_scatter(
        jnp.dot(attn_heads, w_out, preferred_element_type=jnp.float32).astype(jnp.bfloat16),
        "exp",
        scatter_dimension=1,
        tiled=True,
    ).astype(jnp.float32)
    post_cols = (residual.astype(jnp.float32) + attn_cols).astype(jnp.bfloat16)
    post_wide = lax.all_gather(post_cols, "exp", axis=1, tiled=True).astype(jnp.float32)
    mean_square = jnp.mean(post_wide * post_wide, axis=1, keepdims=True)
    moe_rows = (post_wide * lax.rsqrt(mean_square + epsilon) * moe_gain[None, :]).astype(
        jnp.bfloat16
    )
    moe_all = lax.all_gather(moe_rows, "ctx", axis=0, tiled=True)
    packed = jnp.einsum(
        "gjst,gtd->gjsd",
        pick,
        moe_all.reshape(groups, GROUP * block_rows, D),
        preferred_element_type=jnp.float32,
    ).astype(jnp.bfloat16)
    gate_pre = jnp.einsum("gjsd,jdf->gjsf", packed, w_gate, preferred_element_type=jnp.float32)
    up_pre = jnp.einsum("gjsd,jdf->gjsf", packed, w_up, preferred_element_type=jnp.float32)
    hidden = (jax.nn.silu(gate_pre) * up_pre * slot_gate[..., None]).astype(jnp.bfloat16)
    hidden_all = lax.all_gather(hidden, "exp", axis=3, tiled=True)
    expert_out = jnp.einsum(
        "gjsf,jfd->gjsd", hidden_all, w_down, preferred_element_type=jnp.float32
    ).astype(jnp.bfloat16)
    partial = jnp.einsum("gjst,gjsd->gtd", pick, expert_out, preferred_element_type=jnp.float32)
    combined = lax.psum_scatter(
        partial.reshape(columns * block_rows, col_width).astype(jnp.bfloat16),
        "ctx",
        scatter_dimension=0,
        tiled=True,
    )
    return (post_cols.astype(jnp.float32) + combined.astype(jnp.float32)).astype(jnp.bfloat16)


def solution(mesh):
    placed = (
        P("ctx", "exp"),
        P("ctx", "exp"),
        P("ctx", "exp"),
        P("ctx", "exp"),
        P("exp", None),
        P(),
        P("ctx", None),
        P("ctx", None),
        P("ctx", None, "exp"),
        P("ctx", None, "exp"),
        P("ctx", None, "exp"),
    )
    return jax.shard_map(
        local, mesh=mesh, in_specs=placed, out_specs=P("ctx", "exp"), check_vma=False
    )
```

time: 520 us -> 338 us (0.65)
  waiting for transfers between devices: 351 us -> 233 us
  local copies, waits for them, and re-layouts: 51.1 us -> 11.3 us
  other arithmetic: 27.3 us -> 6.84 us
  matrix products: 29.2 us -> 45.2 us
  blocking collectives: 42.9 us -> 27.4 us
    all_gather x2, waiting for transfers between devices: 276 us -> 123 us  [the longest x1 89 us: local(): hidden_all = lax.all_gather(hidden, 'exp', axis=3, tiled=True)]
    reduce_scatter x1 -> x2, waiting for transfers between devices: 15.3 us -> 60.2 us  [the longest x1 36.8 us: local(): lax.psum_scatter(partial.reshape(columns * block_rows, col_width).astype(...]
    all_to_all x1 -> x0, blocking collectives: 32.9 us -> none  [local(): lax.all_to_all(packed.reshape(columns, experts_here, CAP, moe_cols.shape[...]
    all_to_all x1 -> x0, waiting for transfers between devices: 29.3 us -> none  [local(): lax.all_to_all(expert_out, 'ctx', split_axis=0, concat_axis=0, tiled=True)]
    all_gather x0 -> x2, blocking collectives: none -> 27.4 us  [the longest x1 18 us: local(): lax.all_gather(post_cols, 'exp', axis=1, tiled=True).astype(jnp.float32)]
    all_gather x1, waiting for transfers between devices: 9.5 us -> 29.4 us  [local(): lax.all_gather(keys, 'ctx', axis=0, tiled=True)]
    gather x3 -> x0, local copies, waits for them, and re-layouts: 19.8 us -> none  [the longest x2 12.2 us: local(): moe_cols[safe_index]]
    another operation x2 -> x0, other arithmetic: 18.2 us -> none
  transfers between devices with their start and end apart: 6 -> 6, of which waited for: 6 -> 6; matrix products, arithmetic and copies ran while one was open for 7% -> 3% of each run, Pallas kernels for 0% -> 0%
where the time goes in v1:
time: 338 us; the launch traced here: 337 us
  waiting for transfers between devices  233 us (69%)
  matrix products  45.2 us (13%)
  blocking collectives  27.4 us (8%)
  between operations  13.7 us (4%)
  local copies, waits for them, and re-layouts  11.3 us (3%)
  other arithmetic  6.84 us (2%)
    all_gather x1, waiting for transfers between devices, local(): hidden_all = lax.all_gather(hidden, 'exp', axis=3, tiled=True)  89 us
    reduce_scatter x1, waiting for transfers between devices, local(): lax.psum_scatter(partial.reshape(columns * block_rows, col_width).astype(...  36.8 us
    all_gather x1, waiting for transfers between devices, local(): moe_all = lax.all_gather(moe_rows, 'ctx', axis=0, tiled=True)  33.7 us
    all_gather x1, waiting for transfers between devices, local(): lax.all_gather(keys, 'ctx', axis=0, tiled=True)  29.4 us
    reduce_scatter x1, waiting for transfers between devices, local(): lax.psum_scatter(jnp.dot(attn_heads, w_out, preferred_element_type=jnp.fl...  23.4 us
    all_gather x1, waiting for transfers between devices, local(): lax.all_gather(values, 'ctx', axis=0, tiled=True)  18.8 us
    all_gather x1, blocking collectives, local(): lax.all_gather(post_cols, 'exp', axis=1, tiled=True).astype(jnp.float32)  18 us
    dot_general x1, matrix products, local(): jnp.einsum('gjst,gtd->gjsd', pick, moe_all.reshape(groups, GROUP * block_...  10.8 us
  transfers between devices with their start and end apart: 6, of which 6 were waited for; matrix products, arithmetic and copies ran while one was open for 3% of the time, Pallas kernels for 0%

profile of v1, /device:TPU:0, one launch (start us, length us, event | category | flops | bytes accessed | tf_op | source)
XLA Modules:
  0.0 337.4 jit_solution(8109281116101365210)
XLA Ops:
  8.3 29.4 %all-gather.6.cloned.1.call-done = bf16[1536,512]{1,0:T(8,128)(2,1)} async-done(((bf16[192,512]{1,0:T(8,128)(2,1)}), bf16[1536,512]{1,0:T(8,128)(2,1)}) %all-gather.6.cloned.1.call-update) | async-done | bytes 1572880 | tf_op jit(solution)/shard_map/all_gather | solution.py:62
  37.7 2.6 copy.45
  40.3 2.6 fusion.17
  42.9 2.1 copy-done.2
  45.0 1.5 fusion.22
  46.5 18.8 %all-gather.8.cloned.1.call-done = bf16[1536,512]{1,0:T(8,128)(2,1)} async-done(((bf16[192,512]{1,0:T(8,128)(2,1)}), bf16[1536,512]{1,0:T(8,128)(2,1)}) %all-gather.8.cloned.1.call-update) | async-done | bytes 1572880 | tf_op jit(solution)/shard_map/all_gather | solution.py:63
  65.3 2.6 copy.48
  67.8 4.2 %fusion.68 = bf16[4,24,8,128]{3,2,1,0:T(8,128)(2,1)S(1)} fusion(bf16[1536,4,128]{0,2,1:T(8,128)(2,1)} %bitcast.122, f32[4,1536,192]{1,2,0:T(8,128)} %copy-done.2, f32[192,4]{0,1:T(4,128)S(1)} %broadcast_maximum_fusion, pred[192,1536]{1,0:T(8,128)(4,1)S(1)} %iota_compare_fusion, f32[192,4]{0,1:T(4,128)S(1)} %fusion.22), kind=kOutput, calls=%fused_computation.51 | convolution fusion | flops 308084736 | bytes 6789120 | tf_op jit(solution)/shard_map/qhk,khd->qhd/dot_general | solution.py:36
  72.1 1.5 convolution_convert_fusion
  73.7 23.4 %reduce-scatter.3.cloned.1.call-done = bf16[192,512]{1,0:T(8,128)(2,1)} async-done(((bf16[192,2048]{1,0:T(8,128)(2,1)}), bf16[192,512]{1,0:T(8,128)(2,1)}) %reduce-scatter.3.cloned.1.call-update) | async-done | bytes 196624 | tf_op jit(solution)/shard_map/reduce_scatter | solution.py:101
  97.1 1.0 add_convert_fusion.1
  98.1 18.0 %all_gather.21 = bf16[192,2048]{1,0:T(8,128)(2,1)S(1)} all-gather(bf16[192,512]{1,0:T(8,128)(2,1)S(1)} %add_convert_fusion.1), channel_id=1, replica_groups=mesh['ctx'=8,'exp'=4] {'exp'}, dimensions={1}, use_global_device_ids=true | all-gather | bytes 983040 | tf_op jit(solution)/shard_map/all_gather | solution.py:108
  116.3 1.1 fusion.56
  117.6 9.3 %all-gather = f32[8,192,16]{1,2,0:T(8,128)S(1)} all-gather(f32[1,192,16]{1,2,0:T(8,128)S(1)} %maximum_bitcast_fusion), channel_id=1, replica_groups=mesh['ctx'=8,'exp'=4] {'ctx'}, dimensions={0}, use_global_device_ids=true | all-gather | bytes 110592 | tf_op jit(solution)/shard_map/all_gather | solution.py:71
  127.9 0.9 fusion.12
  128.8 33.7 %all-gather.10.cloned.1.call-done = bf16[1536,2048]{1,0:T(8,128)(2,1)} async-done(((bf16[192,2048]{1,0:T(8,128)(2,1)}), bf16[1536,2048]{1,0:T(8,128)(2,1)}) %all-gather.10.cloned.1.call-update) | async-done | bytes 6291472 | tf_op jit(solution)/shard_map/all_gather | solution.py:113
  162.5 10.8 %fusion.13 = bf16[2,8,144,2048]{3,2,1,0:T(8,128)(2,1)S(1)} fusion(bf16[2,768,2048,1]{2,1,3,0:T(8,128)(2,1)} %bitcast.125, f32[2,8,768]{2,1,0:T(8,128)S(1)} %copy.55, f32[144]{0:T(256)S(1)} %iota_convert_fusion), kind=kOutput, calls=%fused_computation.14 | convolution fusion | flops 7254245376 | bytes 15778368 | tf_op jit(solution)/shard_map/gjst,gtd->gjsd/dot_general | solution.py:114
  173.3 3.6 %copy-done.7 = bf16[2,8,144,2048]{3,2,1,0:T(8,128)(2,1)} copy-done((bf16[2,8,144,2048]{3,2,1,0:T(8,128)(2,1)}, bf16[2,8,144,2048]{3,2,1,0:T(8,128)(2,1)S(1)}, u32[]{:S(2)}) %copy-start.7) | copy-done | bytes 9437208
  176.9 5.1 %fusion.6 = f32[8,2,144,256]{3,2,1,0:T(8,128)S(1)} fusion(bf16[8,2048,256]{2,1,0:T(8,128)(2,1)} %param.19, bf16[2,8,144,2048]{3,2,1,0:T(8,128)(2,1)S(1)} %fusion.13), kind=kOutput, calls=%fused_computation.7 | convolution fusion | flops 2415919104 | bytes 20185088 | tf_op jit(solution)/shard_map/gjsd,jdf->gjsf/dot_general | solution.py:120
  182.0 10.1 %fusion.26 = bf16[2,8,144,256]{3,2,0,1:T(8,128)(2,1)} fusion(f32[8,2,144,256]{3,2,1,0:T(8,128)S(1)} %fusion.6, bf16[8,2048,256]{2,1,0:T(8,128)(2,1)} %param.20, bf16[2,8,144,2048]{3,2,1,0:T(8,128)(2,1)} %copy-done.7, f32[2,8,144]{2,0,1:T(2,128)S(1)} %copy.58), kind=kOutput, calls=%fused_computation.30 | convolution fusion | flops 2420047872 | bytes 21373952 | tf_op jit(solution)/shard_map/gjsd,jdf->gjsf/dot_general | solution.py:121
  192.3 89.0 %all-gather.12.cloned.1.call-done = bf16[2,8,144,1024]{3,2,0,1:T(8,128)(2,1)} async-done(((bf16[2,8,144,256]{3,2,0,1:T(8,128)(2,1)}), bf16[2,8,144,1024]{3,2,0,1:T(8,128)(2,1)}) %all-gather.12.cloned.1.call-update) | async-done | bytes 4718608 | tf_op jit(solution)/shard_map/all_gather | solution.py:123
  281.3 10.7 %bitcast_convert_fusion = bf16[2,768,512]{2,1,0:T(8,128)(2,1)} fusion(bf16[8,1024,512]{2,1,0:T(8,128)(2,1)} %param.21, bf16[2,8,144,1024]{3,2,0,1:T(8,128)(2,1)} %all-gather.12.cloned.1.call-done, f32[2,8,768]{2,1,0:T(8,128)S(1)} %copy.55, f32[144]{0:T(256)S(1)} %iota_convert_fusion), kind=kOutput, calls=%fused_computation.25 | convolution fusion | flops 4231593984 | bytes 14729792 | tf_op jit(solution)/shard_map/gjst,gjsd->gtd/dot_general | solution.py:127
  292.1 36.8 %reduce-scatter.5.cloned.1.call-done = bf16[192,512]{1,0:T(8,128)(2,1)} async-done(((bf16[1536,512]{1,0:T(8,128)(2,1)}), bf16[192,512]{1,0:T(8,128)(2,1)}) %reduce-scatter.5.cloned.1.call-update) | async-done | bytes 196624 | tf_op jit(solution)/shard_map/reduce_scatter | solution.py:128
  328.9 1.7 add_convert_fusion
  (48 shorter events, 3.3 us)
Async XLA Ops:
  6.5 65.5 %copy-start = (bf16[512,2048]{1,0:T(8,128)(2,1)S(1)}, bf16[512,2048]{1,0:T(8,128)(2,1)}, u32[]{:S(2)}) copy-start(bf16[512,2048]{1,0:T(8,128)(2,1)} %param.15) | copy-start | bytes 6291460
  6.5 31.1 %all-gather.6.cloned.1.call-start = ((), (), s32[]{:S(2)}) async-start(), calls=%async_computation.2 | async-start | bytes 1769472 | tf_op jit(solution)/shard_map/all_gather | solution.py:62
  7.3 58.0 %all-gather.8.cloned.1.call-start = ((), (), s32[]{:S(2)}) async-start(), calls=%async_computation.3 | async-start | bytes 1769472 | tf_op jit(solution)/shard_map/all_gather | solution.py:63
  8.0 89.1 %reduce-scatter.3.cloned.1.call-start = ((), (), s32[]{:S(2)}) async-start(), calls=%async_computation.4 | async-start | bytes 983040 | tf_op jit(solution)/shard_map/reduce_scatter | solution.py:101
  42.9 2.1 copy-start.2
  67.8 29.2 %copy-start.3 = (bf16[192,512]{1,0:T(8,128)(2,1)S(1)}, bf16[192,512]{1,0:T(8,128)(2,1)}, u32[]{:S(2)}) copy-start(bf16[192,512]{1,0:T(8,128)(2,1)} %param.11) | copy-start | bytes 589828
  72.1 44.3 %copy-start.4 = (f32[2048]{0:T(1024)S(1)}, f32[2048]{0:T(1024)}, u32[]{:S(2)}) copy-start(f32[2048]{0:T(1024)} %param.16) | copy-start | bytes 24580
  72.1 45.5 %copy-start.5 = (s32[192,8]{0,1:T(8,128)S(1)}, s32[192,8]{0,1:T(8,128)}, u32[]{:S(2)}) copy-start(s32[192,8]{0,1:T(8,128)} %param.17) | copy-start | bytes 18436
  72.1 45.5 %copy-start.6 = (f32[192,8]{0,1:T(8,128)S(1)}, f32[192,8]{0,1:T(8,128)}, u32[]{:S(2)}) copy-start(f32[192,8]{0,1:T(8,128)} %param.18) | copy-start | bytes 18436
  73.6 88.9 %all-gather.10.cloned.1.call-start = ((), (), s32[]{:S(2)}) async-start(), calls=%async_computation.5 | async-start | bytes 7077888 | tf_op jit(solution)/shard_map/all_gather | solution.py:113
  117.5 163.9 %all-gather.12.cloned.1.call-start = ((), (), s32[]{:S(2)}) async-start(), calls=%async_computation.6 | async-start | bytes 5898240 | tf_op jit(solution)/shard_map/all_gather | solution.py:123
  173.3 3.6 %copy-start.7 = (bf16[2,8,144,2048]{3,2,1,0:T(8,128)(2,1)}, bf16[2,8,144,2048]{3,2,1,0:T(8,128)(2,1)S(1)}, u32[]{:S(2)}) copy-start(bf16[2,8,144,2048]{3,2,1,0:T(8,128)(2,1)S(1)} %fusion.13) | copy-start | bytes 28311556
  192.0 136.9 %reduce-scatter.5.cloned.1.call-start = ((), (), s32[]{:S(2)}) async-start(), calls=%async_computation.7 | async-start | bytes 1769472 | tf_op jit(solution)/shard_map/reduce_scatter | solution.py:128
  281.3 49.2 %copy-start.1 = (bf16[512,2048]{1,0:T(8,128)(2,1)S(1)}, bf16[512,2048]{1,0:T(8,128)(2,1)}, u32[]{:S(2)}) copy-start(bf16[512,2048]{1,0:T(8,128)(2,1)} %param.15) | copy-start | bytes 6291460
Sparse Core Ops, SparseCore 0:
  9.2 28.3 all-gather.5
  39.6 25.6 all-gather.7
  73.8 23.2 reduce-scatter.2
  117.6 44.8 all-gather.9
  192.2 89.1 all-gather.11
  292.2 36.6 reduce-scatter.4

commit v2 on v1

--- a/solution.py
+++ b/solution.py
@@ -1,8 +1,11 @@
+import functools
 import math
 
 import jax
 import jax.numpy as jnp
 from jax import lax
+from jax.experimental import pallas as pl
+from jax.experimental.pallas import tpu as pltpu
 from jax.sharding import PartitionSpec as P
 
 D = 2048
@@ -10,9 +13,291 @@
 K = 8
 CAP = 36
 GROUP = 4
+LAG = 2
+MESH = pl.DeviceIdType.MESH
 
 
 epsilon = 1e-05
+
+
+def gather_kernel(n, k_ref, v_ref, ko_ref, vo_ref, own_sem, far_send, far_recv, sib_send, sib_recv):
+    me = lax.axis_index("ctx")
+    core, chip, chips = lax.rem(me, 2), me // 2, n // 2
+    rows = k_ref.shape[0]
+    sibling = chip * 2 + 1 - core
+    peers = [lax.rem(chip + d, chips) * 2 + core for d in range(1, chips)]
+    barrier = pltpu.get_barrier_semaphore()
+    for other in [sibling] + peers:
+        pl.semaphore_signal(barrier, inc=1, device_id={"ctx": other}, device_id_type=MESH)
+    pl.semaphore_wait(barrier, chips)
+
+    def block(ref, index):
+        return ref.at[pl.ds(pl.multiple_of(index * rows, rows), rows)]
+
+    pairs = ((k_ref, ko_ref), (v_ref, vo_ref))
+    far, near, own = [], [], []
+    for a, (src, dst) in enumerate(pairs):
+        for d, peer in enumerate(peers):
+            copy = pltpu.make_async_remote_copy(
+                src_ref=src,
+                dst_ref=block(dst, me),
+                send_sem=far_send.at[a, d],
+                recv_sem=far_recv.at[a, d],
+                device_id={"ctx": peer},
+                device_id_type=MESH,
+            )
+            copy.start()
+            far.append((a, d, copy))
+    for a, (src, dst) in enumerate(pairs):
+        copy = pltpu.make_async_remote_copy(
+            src_ref=src,
+            dst_ref=block(dst, me),
+            send_sem=sib_send.at[a, chips - 1],
+            recv_sem=sib_recv.at[a, chips - 1],
+            device_id={"ctx": sibling},
+            device_id_type=MESH,
+        )
+        copy.start()
+        near.append(copy)
+        copy = pltpu.make_async_copy(src, block(dst, me), own_sem.at[a])
+        copy.start()
+        own.append(copy)
+    for a, d, copy in far:
+        copy.wait_recv()
+        origin = lax.rem(chip + chips - d - 1, chips) * 2 + core
+        dst = pairs[a][1]
+        onward = pltpu.make_async_remote_copy(
+            src_ref=block(dst, origin),
+            dst_ref=block(dst, origin),
+            send_sem=sib_send.at[a, d],
+            recv_sem=sib_recv.at[a, d],
+            device_id={"ctx": sibling},
+            device_id_type=MESH,
+        )
+        onward.start()
+        near.append(onward)
+    for copy in own:
+        copy.wait()
+    for _, _, copy in far:
+        copy.wait_send()
+    for copy in near:
+        copy.wait()
+
+
+def gather_keys_values(keys, values, n):
+    rows, width = keys.shape
+    full = jax.ShapeDtypeStruct((n * rows, width), keys.dtype)
+    return pl.pallas_call(
+        functools.partial(gather_kernel, n),
+        out_shape=(full, full),
+        in_specs=[pl.BlockSpec(memory_space=pl.ANY)] * 2,
+        out_specs=[pl.BlockSpec(memory_space=pl.ANY)] * 2,
+        scratch_shapes=[
+            pltpu.SemaphoreType.DMA((2,)),
+            pltpu.SemaphoreType.DMA((2, n // 2)),
+            pltpu.SemaphoreType.DMA((2, n // 2)),
+            pltpu.SemaphoreType.DMA((2, n // 2)),
+            pltpu.SemaphoreType.DMA((2, n // 2)),
+        ],
+        compiler_params=pltpu.CompilerParams(collective_id=1, has_side_effects=True),
+        cost_estimate=pl.CostEstimate(flops=0, bytes_accessed=60_000_000, transcendentals=0),
+    )(keys, values)
+
+
+def expert_kernel(n, count, x_ref, g_ref, wg_ref, wu_ref, wd_ref, out_ref, held, send, recv):
+    me = lax.axis_index("exp")
+    step = pl.program_id(0)
+    groups, _, slots, width = x_ref.shape
+    rows = groups * slots
+    units = wg_ref.shape[2]
+    has_left, has_right = me > 0, me < n - 1
+
+    def hop(side, source, expert):
+        return pltpu.make_async_remote_copy(
+            src_ref=held.at[source, expert],
+            dst_ref=held.at[source, expert],
+            send_sem=send.at[side, source, expert],
+            recv_sem=recv.at[source, expert],
+            device_id={"exp": me + 1 if side else me - 1},
+            device_id_type=MESH,
+        )
+
+    barrier = pltpu.get_barrier_semaphore()
+
+    @pl.when(step == 0)
+    def _():
+        for side, there in ((0, has_left), (1, has_right)):
+
+            @pl.when(there)
+            def _():
+                pl.semaphore_signal(
+                    barrier,
+                    inc=1,
+                    device_id={"exp": me + 1 if side else me - 1},
+                    device_id_type=MESH,
+                )
+
+        pl.semaphore_wait(barrier, jnp.minimum(me, 1) + jnp.minimum(n - 1 - me, 1))
+
+    @pl.when(step < count)
+    def _():
+        x = x_ref[...].reshape(rows, width)
+        gate = jnp.dot(x, wg_ref[0], preferred_element_type=jnp.float32)
+        up = jnp.dot(x, wu_ref[0], preferred_element_type=jnp.float32)
+        hidden = gate / (1.0 + jnp.exp(-gate)) * up * g_ref[0]
+        held[me, step] = hidden.astype(jnp.bfloat16)
+        for side, there in ((0, has_left), (1, has_right)):
+
+            @pl.when(there)
+            def _():
+                hop(side, me, step).start()
+
+    for distance in range(1, n):
+        expert = step - LAG * distance
+        for side in (0, 1):
+            source = me + distance if side == 0 else me - distance
+            onward = has_left if side == 0 else has_right
+            inside = (source < n) if side == 0 else (source >= 0)
+
+            @pl.when((expert >= 0) & (expert < count) & inside)
+            def _():
+                hop(side, source, expert).wait_recv()
+
+                @pl.when(onward)
+                def _():
+                    hop(side, source, expert).start()
+
+    done = step - LAG * (n - 1)
+
+    @pl.when(done >= 0)
+    def _():
+        total = jnp.zeros((rows, wd_ref.shape[2]), jnp.float32)
+        for source in range(n):
+            total += jnp.dot(
+                held[source, done],
+                wd_ref[0, source * units : (source + 1) * units],
+                preferred_element_type=jnp.float32,
+            )
+        out_ref[...] = total.astype(jnp.bfloat16).reshape(out_ref.shape)
+
+    @pl.when(done == count - 1)
+    def _():
+        for source in range(n):
+            for side, there in (
+                (0, has_left & (me <= source)),
+                (1, has_right & (me >= source)),
+            ):
+
+                @pl.when(there)
+                def _():
+                    @pl.loop(0, count)
+                    def _(expert):
+                        hop(side, source, expert).wait_send()
+
+
+def run_experts(packed, slot_gate, w_gate, w_up, w_down, n):
+    groups, count, slots, width = packed.shape
+    rows = groups * slots
+    units, hidden, columns = w_gate.shape[2], w_down.shape[1], w_down.shape[2]
+    late = LAG * (n - 1)
+
+    def first(step):
+        return jnp.minimum(step, count - 1)
+
+    def second(step):
+        return jnp.maximum(step - late, 0)
+
+    return pl.pallas_call(
+        functools.partial(expert_kernel, n, count),
+        grid=(count + late,),
+        out_shape=jax.ShapeDtypeStruct((groups, count, slots, columns), jnp.bfloat16),
+        in_specs=[
+            pl.BlockSpec((groups, 1, slots, width), lambda i: (0, first(i), 0, 0)),
+            pl.BlockSpec((1, rows, 1), lambda i: (first(i), 0, 0)),
+            pl.BlockSpec((1, width, units), lambda i: (first(i), 0, 0)),
+            pl.BlockSpec((1, width, units), lambda i: (first(i), 0, 0)),
+            pl.BlockSpec((1, hidden, columns), lambda i: (second(i), 0, 0)),
+        ],
+        out_specs=pl.BlockSpec((groups, 1, slots, columns), lambda i: (0, second(i), 0, 0)),
+        scratch_shapes=[
+            pltpu.VMEM((n, count, rows, units), jnp.bfloat16),
+            pltpu.SemaphoreType.DMA((2, n, count)),
+            pltpu.SemaphoreType.DMA((n, count)),
+        ],
+        compiler_params=pltpu.CompilerParams(
+            collective_id=2, has_side_effects=True, vmem_limit_bytes=40 * 1024 * 1024
+        ),
+        cost_estimate=pl.CostEstimate(
+            flops=8_000_000_000, bytes_accessed=100_000_000, transcendentals=0
+        ),
+    )(packed, slot_gate, w_gate, w_up, w_down)
+
+
+def scatter_kernel(n, part_ref, out_ref, near, stage, far, near_send, near_recv, send, recv):
+    me = lax.axis_index("ctx")
+    core, chip, chips = lax.rem(me, 2), me // 2, n // 2
+    sibling = chip * 2 + 1 - core
+    barrier = pltpu.get_barrier_semaphore()
+    for other in [sibling] + [lax.rem(chip + d, chips) * 2 + core for d in range(1, chips)]:
+        pl.semaphore_signal(barrier, inc=1, device_id={"ctx": other}, device_id_type=MESH)
+    pl.semaphore_wait(barrier, chips)
+
+    def pass_over(d):
+        target = lax.rem(chip + d, chips)
+        return pltpu.make_async_remote_copy(
+            src_ref=part_ref.at[target * 2 + 1 - core],
+            dst_ref=near.at[d],
+            send_sem=near_send.at[d],
+            recv_sem=near_recv.at[d],
+            device_id={"ctx": sibling},
+            device_id_type=MESH,
+        )
+
+    def send_off(d):
+        return pltpu.make_async_remote_copy(
+            src_ref=stage.at[d],
+            dst_ref=far.at[d],
+            send_sem=send.at[d],
+            recv_sem=recv.at[d],
+            device_id={"ctx": lax.rem(chip + d, chips) * 2 + core},
+            device_id_type=MESH,
+        )
+
+    order = list(range(1, chips)) + [0]
+    for d in order:
+        pass_over(d).start()
+    for d in order:
+        pass_over(d).wait_recv()
+        mine = part_ref[lax.rem(chip + d, chips) * 2 + core].astype(jnp.float32)
+        both = mine + near[d].astype(jnp.float32)
+        if d:
+            stage[d] = both.astype(jnp.bfloat16)
+            send_off(d).start()
+        else:
+            out_ref[...] = both
+    for d in range(1, chips):
+        send_off(d).wait_recv()
+        out_ref[...] += far[d].astype(jnp.float32)
+    for d in range(1, chips):
+        send_off(d).wait_send()
+    for d in order:
+        pass_over(d).wait_send()
+
+
+def scatter_sum(part, n):
+    _, rows, width = part.shape
+    half = pltpu.VMEM((n // 2, rows, width), jnp.bfloat16)
+    sems = pltpu.SemaphoreType.DMA((n // 2,))
+    return pl.pallas_call(
+        functools.partial(scatter_kernel, n),
+        out_shape=jax.ShapeDtypeStruct((rows, width), jnp.float32),
+        in_specs=[pl.BlockSpec(memory_space=pltpu.VMEM)],
+        out_specs=pl.BlockSpec(memory_space=pltpu.VMEM),
+        scratch_shapes=[half, half, half, sems, sems, sems, sems],
+        compiler_params=pltpu.CompilerParams(
+            collective_id=3, has_side_effects=True, vmem_limit_bytes=40 * 1024 * 1024
+        ),
+    )(part)
 
 
 def attend(carried, pieces, q_three, query_pos):
@@ -58,10 +343,7 @@
     )
     row_max, row_total, row_accum = attend(
         start_state,
-        (
-            lax.all_gather(keys, "ctx", axis=0, tiled=True),
-            lax.all_gather(values, "ctx", axis=0, tiled=True),
-        ),
+        gather_keys_values(keys, values, columns),
         q_three,
         query_pos,
     )
@@ -117,21 +399,13 @@
         moe_all.reshape(groups, GROUP * block_rows, D),
         preferred_element_type=jnp.float32,
     ).astype(jnp.bfloat16)
-    gate_pre = jnp.einsum("gjsd,jdf->gjsf", packed, w_gate, preferred_element_type=jnp.float32)
-    up_pre = jnp.einsum("gjsd,jdf->gjsf", packed, w_up, preferred_element_type=jnp.float32)
-    hidden = (jax.nn.silu(gate_pre) * up_pre * slot_gate[..., None]).astype(jnp.bfloat16)
-    hidden_all = lax.all_gather(hidden, "exp", axis=3, tiled=True)
-    expert_out = jnp.einsum(
-        "gjsf,jfd->gjsd", hidden_all, w_down, preferred_element_type=jnp.float32
-    ).astype(jnp.bfloat16)
+    gate_column = slot_gate.transpose(1, 0, 2).reshape(experts_here, groups * GROUP * CAP, 1)
+    expert_out = run_experts(packed, gate_column, w_gate, w_up, w_down, lax.axis_size("exp"))
     partial = jnp.einsum("gjst,gjsd->gtd", pick, expert_out, preferred_element_type=jnp.float32)
-    combined = lax.psum_scatter(
-        partial.reshape(columns * block_rows, col_width).astype(jnp.bfloat16),
-        "ctx",
-        scatter_dimension=0,
-        tiled=True,
-    )
-    return (post_cols.astype(jnp.float32) + combined.astype(jnp.float32)).astype(jnp.bfloat16)
+    combined = scatter_sum(
+        partial.astype(jnp.bfloat16).reshape(columns, block_rows, col_width), columns
+    )
+    return (post_cols.astype(jnp.float32) + combined).astype(jnp.bfloat16)
 
 
 def solution(mesh):

time: 338 us -> 251 us (0.74)
  waiting for transfers between devices: 233 us -> 57.5 us
  Pallas kernels: 0 us -> 121 us
  matrix products: 45.2 us -> 20.6 us
  local copies, waits for them, and re-layouts: 11.3 us -> 4.39 us
    all_gather x3 -> x0, waiting for transfers between devices: 137 us -> none  [the longest x1 89 us: local(): hidden_all = lax.all_gather(hidden, 'exp', axis=3, tiled=True)]
    pallas_call x0 -> x3, Pallas kernels: none -> 121 us  [the longest x1 83.8 us: run_experts(): pl.pallas_call(functools.partial(expert_kernel, n, count), grid=(count +...]
    reduce_scatter x1 -> x0, waiting for transfers between devices: 36.8 us -> none  [local(): lax.psum_scatter(partial.reshape(columns * block_rows, col_width).astype(...]
    dot_general x2 -> x0, matrix products: 15.1 us -> none  [the longest x1 10.1 us: local(): jnp.einsum('gjsd,jdf->gjsf', packed, w_up, preferred_element_type=jnp.flo...]
    dot_general x1, matrix products: 10.7 us -> 2.31 us  [local(): jnp.einsum('gjst,gjsd->gtd', pick, expert_out, preferred_element_type=jnp...]
    all_gather x2 -> x0, local copies, waits for them, and re-layouts: 5.15 us -> none  [the longest x1 2.58 us: local(): lax.all_gather(keys, 'ctx', axis=0, tiled=True)]
  transfers between devices with their start and end apart: 6 -> 2, of which waited for: 6 -> 2; matrix products, arithmetic and copies ran while one was open for 3% -> 1% of each run, Pallas kernels for 0% -> 0%
where the time goes in v2:
time: 251 us
  Pallas kernels  121 us (48%)
  waiting for transfers between devices  57.5 us (23%)
  blocking collectives  27.4 us (11%)
  matrix products  20.6 us (8%)
  between operations  13.7 us (5%)
  other arithmetic  5.91 us (2%)
  local copies, waits for them, and re-layouts  4.39 us (2%)
    pallas_call x1, Pallas kernels, run_experts(): pl.pallas_call(functools.partial(expert_kernel, n, count), grid=(count +...  83.8 us
    all_gather x1, waiting for transfers between devices, local(): moe_all = lax.all_gather(moe_rows, 'ctx', axis=0, tiled=True)  33.1 us
    reduce_scatter x1, waiting for transfers between devices, local(): lax.psum_scatter(jnp.dot(attn_heads, w_out, preferred_element_type=jnp.fl...  24.3 us
    pallas_call x1, Pallas kernels, gather_keys_values(): pl.pallas_call(functools.partial(gather_kernel, n), out_shape=(full, full...  24.1 us
    all_gather x1, blocking collectives, local(): lax.all_gather(post_cols, 'exp', axis=1, tiled=True).astype(jnp.float32)  18 us
    pallas_call x1, Pallas kernels, scatter_sum(): pl.pallas_call(functools.partial(scatter_kernel, n), out_shape=jax.ShapeD...  13.3 us
    dot_general x1, matrix products, local(): jnp.einsum('gjst,gtd->gjsd', pick, moe_all.reshape(groups, GROUP * block_...  12.4 us
    all_gather x1, blocking collectives, local(): lax.all_gather(jnp.concatenate([expert_ids.astype(jnp.float32), gate_weig...  9.36 us
  transfers between devices with their start and end apart: 2, of which 2 were waited for; matrix products, arithmetic and copies ran while one was open for 1% of the time, Pallas kernels for 0%

profile of v2, /device:TPU:0, one launch (start us, length us, event | category | flops | bytes accessed | tf_op | source)
XLA Modules:
  0.0 250.7 jit_solution(12270597388116211892)
XLA Ops:
  6.5 0.2 iota_compare_fusion
  6.8 24.1 %shard_map.109 = (bf16[1536,512]{1,0:T(8,128)(2,1)}, bf16[1536,512]{1,0:T(8,128)(2,1)}) custom-call(bf16[192,512]{1,0:T(8,128)(2,1)} %k_ref.1, bf16[192,512]{1,0:T(8,128)(2,1)} %v_ref.1), custom_call_target="tpu_custom_call" | custom-call | bytes 60000000 | tf_op jit(solution)/shard_map/pallas_call | solution.py:90
  30.9 2.7 %fusion.8 = (f32[192,4]{0,1:T(4,128)S(1)}, f32[4,1536,192]{1,2,0:T(8,128)S(1)}) fusion(pred[192,1536]{1,0:T(8,128)(4,1)S(1)} %iota_compare_fusion, bf16[1536,512]{1,0:T(8,128)(2,1)} %get-tuple-element.8, bf16[192,512]{1,0:T(8,128)(2,1)} %param.12), kind=kOutput, calls=%fused_computation.9 | convolution fusion | flops 305528064 | bytes 6786048 | tf_op jit(solution)/shard_map/qhd,khd->qhk/dot_general | solution.py:313
  33.6 1.5 fusion.13
  35.1 1.6 fusion.45
  36.7 1.5 convolution_convert_fusion
  38.3 24.3 %reduce-scatter.2.cloned.1.call-done = bf16[192,512]{1,0:T(8,128)(2,1)} async-done(((bf16[192,2048]{1,0:T(8,128)(2,1)}), bf16[192,512]{1,0:T(8,128)(2,1)}) %reduce-scatter.2.cloned.1.call-update) | async-done | bytes 196624 | tf_op jit(solution)/shard_map/reduce_scatter | solution.py:383
  62.6 1.0 add_convert_fusion.1
  63.6 18.0 %all_gather.10 = bf16[192,2048]{1,0:T(8,128)(2,1)S(1)} all-gather(bf16[192,512]{1,0:T(8,128)(2,1)S(1)} %add_convert_fusion.1), channel_id=1, replica_groups=mesh['ctx'=8,'exp'=4] {'exp'}, dimensions={1}, use_global_device_ids=true | all-gather | bytes 983040 | tf_op jit(solution)/shard_map/all_gather | solution.py:390
  81.6 0.2 fusion.20
  81.8 1.1 fusion.22
  83.0 9.4 %all-gather = f32[8,192,16]{1,2,0:T(8,128)S(1)} all-gather(f32[1,192,16]{1,2,0:T(8,128)S(1)} %maximum_bitcast_fusion), channel_id=1, replica_groups=mesh['ctx'=8,'exp'=4] {'ctx'}, dimensions={0}, use_global_device_ids=true | all-gather | bytes 110592 | tf_op jit(solution)/shard_map/all_gather | solution.py:353
  92.6 0.1 compare_reduce_fusion
  92.8 0.2 fusion.34
  93.2 0.1 fusion.50
  93.3 0.9 fusion.4
  94.2 0.6 reshape.102.g_ref
  94.8 33.1 %all-gather.3.cloned.1.call-done = bf16[1536,2048]{1,0:T(8,128)(2,1)} async-done(((bf16[192,2048]{1,0:T(8,128)(2,1)}), bf16[1536,2048]{1,0:T(8,128)(2,1)}) %all-gather.3.cloned.1.call-update) | async-done | bytes 6291472 | tf_op jit(solution)/shard_map/all_gather | solution.py:395
  127.9 12.4 %fusion.5.x_ref = bf16[2,8,144,2048]{3,2,1,0:T(8,128)(2,1)} fusion(bf16[2,768,2048,1]{2,1,3,0:T(8,128)(2,1)} %bitcast.101, f32[2,8,768]{2,1,0:T(8,128)S(1)} %copy.48, f32[144]{0:T(256)S(1)} %iota_convert_fusion), kind=kOutput, calls=%fused_computation.6 | convolution fusion | flops 7254245376 | bytes 15778368 | tf_op jit(solution)/shard_map/gjst,gtd->gjsd/dot_general | solution.py:396
  140.3 3.4 %copy-done.1 = bf16[8,2048,256]{2,1,0:T(8,128)(2,1)S(1)} copy-done((bf16[8,2048,256]{2,1,0:T(8,128)(2,1)S(1)}, bf16[8,2048,256]{2,1,0:T(8,128)(2,1)}, u32[]{:S(2)}) %copy-start.1) | copy-done | bytes 8388632
  143.7 83.8 %shard_map.110 = bf16[2,8,144,512]{3,2,1,0:T(8,128)(2,1)S(1)} custom-call(bf16[2,8,144,2048]{3,2,1,0:T(8,128)(2,1)} %fusion.5.x_ref, f32[8,288,1]{2,1,0:T(8,128)S(1)} %reshape.102.g_ref, bf16[8,2048,256]{2,1,0:T(8,128)(2,1)S(1)} %copy-done.1, bf16[8,2048,256]{2,1,0:T(8,128)(2,1)} %wu_ref.1, bf16[8,1024,512]{2,1,0:T(8,128)(2,1)} %wd_ref.1), custom_call_target="tpu_custom_call" | custom-call | flops 8000000000 | bytes 100000000 | tf_op jit(solution)/shard_map/pallas_call | solution.py:210
  227.5 2.3 bitcast_convert_fusion
  229.8 13.3 %shard_map.111 = f32[192,512]{1,0:T(8,128)S(1)} custom-call(bf16[8,192,512]{2,1,0:T(8,128)(2,1)S(1)} %bitcast.97), custom_call_target="tpu_custom_call" | custom-call | tf_op jit(solution)/shard_map/pallas_call | solution.py:291
  243.1 0.7 add_convert_fusion
  (34 shorter events, 0.6 us)
Async XLA Ops:
  6.5 30.1 %copy-start = (bf16[512,2048]{1,0:T(8,128)(2,1)S(1)}, bf16[512,2048]{1,0:T(8,128)(2,1)}, u32[]{:S(2)}) copy-start(bf16[512,2048]{1,0:T(8,128)(2,1)} %param.15) | copy-start | bytes 6291460
  6.5 56.0 %reduce-scatter.2.cloned.1.call-start = ((), (), s32[]{:S(2)}) async-start(), calls=%async_computation.1 | async-start | bytes 983040 | tf_op jit(solution)/shard_map/reduce_scatter | solution.py:383
  30.9 4.2 %copy-start.6 = (bf16[1536,512]{1,0:T(8,128)(2,1)S(1)}, bf16[1536,512]{1,0:T(8,128)(2,1)}, u32[]{:S(2)}) copy-start(bf16[1536,512]{1,0:T(8,128)(2,1)} %get-tuple-element.7) | copy-start | bytes 4718596
  35.1 27.5 %copy-start.2 = (bf16[192,512]{1,0:T(8,128)(2,1)S(1)}, bf16[192,512]{1,0:T(8,128)(2,1)}, u32[]{:S(2)}) copy-start(bf16[192,512]{1,0:T(8,128)(2,1)} %param.11) | copy-start | bytes 589828
  36.7 45.1 %copy-start.3 = (f32[2048]{0:T(1024)S(1)}, f32[2048]{0:T(1024)}, u32[]{:S(2)}) copy-start(f32[2048]{0:T(1024)} %param.16) | copy-start | bytes 24580
  36.7 46.3 %copy-start.4 = (s32[192,8]{0,1:T(8,128)S(1)}, s32[192,8]{0,1:T(8,128)}, u32[]{:S(2)}) copy-start(s32[192,8]{0,1:T(8,128)} %param.17) | copy-start | bytes 18436
  36.7 46.3 %copy-start.5 = (f32[192,8]{0,1:T(8,128)S(1)}, f32[192,8]{0,1:T(8,128)}, u32[]{:S(2)}) copy-start(f32[192,8]{0,1:T(8,128)} %param.18) | copy-start | bytes 18436
  38.2 89.7 %all-gather.3.cloned.1.call-start = ((), (), s32[]{:S(2)}) async-start(), calls=%async_computation.2 | async-start | bytes 7077888 | tf_op jit(solution)/shard_map/all_gather | solution.py:395
  140.3 3.4 %copy-start.1 = (bf16[8,2048,256]{2,1,0:T(8,128)(2,1)S(1)}, bf16[8,2048,256]{2,1,0:T(8,128)(2,1)}, u32[]{:S(2)}) copy-start(bf16[8,2048,256]{2,1,0:T(8,128)(2,1)} %wg_ref.1) | copy-start | bytes 25165828
Sparse Core Ops, SparseCore 0:
  38.3 24.2 reduce-scatter.1
  83.1 44.8 all-gather.2

commit v3 on v2

--- a/solution.py
+++ b/solution.py
@@ -20,7 +20,20 @@
 epsilon = 1e-05
 
 
-def gather_kernel(n, k_ref, v_ref, ko_ref, vo_ref, own_sem, far_send, far_recv, sib_send, sib_recv):
+def gather_kernel(
+    n,
+    k_ref,
+    v_ref,
+    r_ref,
+    ko_ref,
+    vo_ref,
+    ro_ref,
+    own_sem,
+    far_send,
+    far_recv,
+    sib_send,
+    sib_recv,
+):
     me = lax.axis_index("ctx")
     core, chip, chips = lax.rem(me, 2), me // 2, n // 2
     rows = k_ref.shape[0]
@@ -34,7 +47,7 @@
     def block(ref, index):
         return ref.at[pl.ds(pl.multiple_of(index * rows, rows), rows)]
 
-    pairs = ((k_ref, ko_ref), (v_ref, vo_ref))
+    pairs = ((k_ref, ko_ref), (v_ref, vo_ref), (r_ref, ro_ref))
     far, near, own = [], [], []
     for a, (src, dst) in enumerate(pairs):
         for d, peer in enumerate(peers):
@@ -84,30 +97,28 @@
         copy.wait()
 
 
-def gather_keys_values(keys, values, n):
-    rows, width = keys.shape
-    full = jax.ShapeDtypeStruct((n * rows, width), keys.dtype)
+def gather_blocks(arrays, n):
     return pl.pallas_call(
         functools.partial(gather_kernel, n),
-        out_shape=(full, full),
-        in_specs=[pl.BlockSpec(memory_space=pl.ANY)] * 2,
-        out_specs=[pl.BlockSpec(memory_space=pl.ANY)] * 2,
+        out_shape=[jax.ShapeDtypeStruct((n * a.shape[0], a.shape[1]), a.dtype) for a in arrays],
+        in_specs=[pl.BlockSpec(memory_space=pl.ANY)] * 3,
+        out_specs=[pl.BlockSpec(memory_space=pl.ANY)] * 3,
         scratch_shapes=[
-            pltpu.SemaphoreType.DMA((2,)),
-            pltpu.SemaphoreType.DMA((2, n // 2)),
-            pltpu.SemaphoreType.DMA((2, n // 2)),
-            pltpu.SemaphoreType.DMA((2, n // 2)),
-            pltpu.SemaphoreType.DMA((2, n // 2)),
+            pltpu.SemaphoreType.DMA((3,)),
+            pltpu.SemaphoreType.DMA((3, n // 2)),
+            pltpu.SemaphoreType.DMA((3, n // 2)),
+            pltpu.SemaphoreType.DMA((3, n // 2)),
+            pltpu.SemaphoreType.DMA((3, n // 2)),
         ],
         compiler_params=pltpu.CompilerParams(collective_id=1, has_side_effects=True),
         cost_estimate=pl.CostEstimate(flops=0, bytes_accessed=60_000_000, transcendentals=0),
-    )(keys, values)
-
-
-def expert_kernel(n, count, x_ref, g_ref, wg_ref, wu_ref, wd_ref, out_ref, held, send, recv):
+    )(*arrays)
+
+
+def expert_kernel(n, count, pick_ref, all_ref, g_ref, wg_ref, wu_ref, wd_ref, out_ref, held, send, recv):
     me = lax.axis_index("exp")
     step = pl.program_id(0)
-    groups, _, slots, width = x_ref.shape
+    groups, _, slots, _ = pick_ref.shape
     rows = groups * slots
     units = wg_ref.shape[2]
     has_left, has_right = me > 0, me < n - 1
@@ -141,7 +152,15 @@
 
     @pl.when(step < count)
     def _():
-        x = x_ref[...].reshape(rows, width)
+        x = jnp.concatenate(
+            [
+                jnp.dot(pick_ref[g, 0], all_ref[g], preferred_element_type=jnp.float32).astype(
+                    jnp.bfloat16
+                )
+                for g in range(groups)
+            ],
+            axis=0,
+        )
         gate = jnp.dot(x, wg_ref[0], preferred_element_type=jnp.float32)
         up = jnp.dot(x, wu_ref[0], preferred_element_type=jnp.float32)
         hidden = gate / (1.0 + jnp.exp(-gate)) * up * g_ref[0]
@@ -195,8 +214,9 @@
                         hop(side, source, expert).wait_send()
 
 
-def run_experts(packed, slot_gate, w_gate, w_up, w_down, n):
-    groups, count, slots, width = packed.shape
+def run_experts(pick, moe_all, slot_gate, w_gate, w_up, w_down, n):
+    groups, count, slots, tokens = pick.shape
+    width = moe_all.shape[2]
     rows = groups * slots
     units, hidden, columns = w_gate.shape[2], w_down.shape[1], w_down.shape[2]
     late = LAG * (n - 1)
@@ -212,7 +232,10 @@
         grid=(count + late,),
         out_shape=jax.ShapeDtypeStruct((groups, count, slots, columns), jnp.bfloat16),
         in_specs=[
-            pl.BlockSpec((groups, 1, slots, width), lambda i: (0, first(i), 0, 0)),
+            pl.BlockSpec((groups, 1, slots, tokens), lambda i: (0, first(i), 0, 0)),
+            pl.BlockSpec(
+                (groups, tokens, width), lambda i: (0, 0, 0), pipeline_mode=pl.Buffered(1)
+            ),
             pl.BlockSpec((1, rows, 1), lambda i: (first(i), 0, 0)),
             pl.BlockSpec((1, width, units), lambda i: (first(i), 0, 0)),
             pl.BlockSpec((1, width, units), lambda i: (first(i), 0, 0)),
@@ -225,12 +248,12 @@
             pltpu.SemaphoreType.DMA((n, count)),
         ],
         compiler_params=pltpu.CompilerParams(
-            collective_id=2, has_side_effects=True, vmem_limit_bytes=40 * 1024 * 1024
+            collective_id=2, has_side_effects=True, vmem_limit_bytes=56 * 1024 * 1024
         ),
         cost_estimate=pl.CostEstimate(
             flops=8_000_000_000, bytes_accessed=100_000_000, transcendentals=0
         ),
-    )(packed, slot_gate, w_gate, w_up, w_down)
+    )(pick, moe_all, slot_gate, w_gate, w_up, w_down)
 
 
 def scatter_kernel(n, part_ref, out_ref, near, stage, far, near_send, near_recv, send, recv):
@@ -341,20 +364,18 @@
         jnp.zeros((block_rows, heads_here), jnp.float32),
         jnp.zeros((block_rows, heads_here, head_dim), jnp.float32),
     )
+    keys_all, values_all, routing = gather_blocks(
+        (keys, values, jnp.concatenate([expert_ids.astype(jnp.float32), gate_weights], axis=1)),
+        columns,
+    )
     row_max, row_total, row_accum = attend(
         start_state,
-        gather_keys_values(keys, values, columns),
+        (keys_all, values_all),
         q_three,
         query_pos,
     )
     attn_heads = (
         (row_accum / row_total[:, :, None]).reshape(block_rows, col_width).astype(jnp.bfloat16)
-    )
-    routing = lax.all_gather(
-        jnp.concatenate([expert_ids.astype(jnp.float32), gate_weights], axis=1),
-        "ctx",
-        axis=0,
-        tiled=True,
     )
     here = (ctx_index * experts_here + jnp.arange(experts_here, dtype=jnp.int32)).astype(
         jnp.float32
@@ -393,14 +414,16 @@
         jnp.bfloat16
     )
     moe_all = lax.all_gather(moe_rows, "ctx", axis=0, tiled=True)
-    packed = jnp.einsum(
-        "gjst,gtd->gjsd",
+    gate_column = slot_gate.transpose(1, 0, 2).reshape(experts_here, groups * GROUP * CAP, 1)
+    expert_out = run_experts(
         pick,
         moe_all.reshape(groups, GROUP * block_rows, D),
-        preferred_element_type=jnp.float32,
-    ).astype(jnp.bfloat16)
-    gate_column = slot_gate.transpose(1, 0, 2).reshape(experts_here, groups * GROUP * CAP, 1)
-    expert_out = run_experts(packed, gate_column, w_gate, w_up, w_down, lax.axis_size("exp"))
+        gate_column,
+        w_gate,
+        w_up,
+        w_down,
+        lax.axis_size("exp"),
+    )
     partial = jnp.einsum("gjst,gjsd->gtd", pick, expert_out, preferred_element_type=jnp.float32)
     combined = scatter_sum(
         partial.astype(jnp.bfloat16).reshape(columns, block_rows, col_width), columns

time: 251 us -> 247 us (0.984)
  matrix products: 20.6 us -> 9.76 us
  blocking collectives: 27.4 us -> 18.2 us
  Pallas kernels: 121 us -> 129 us
  other arithmetic: 5.91 us -> 10.1 us
    dot_general x1 -> x0, matrix products: 12.4 us -> none  [local(): jnp.einsum('gjst,gtd->gjsd', pick, moe_all.reshape(groups, GROUP * block_...]
    all_gather x1 -> x0, blocking collectives: 9.36 us -> none  [local(): lax.all_gather(jnp.concatenate([expert_ids.astype(jnp.float32), gate_weig...]
    pallas_call x1, Pallas kernels: 24.1 us -> 28.2 us  [gather_blocks(): pl.pallas_call(functools.partial(gather_kernel, n), out_shape=[jax.ShapeD...]
    pallas_call x1, Pallas kernels: 83.8 us -> 87.5 us  [run_experts(): pl.pallas_call(functools.partial(expert_kernel, n, count), grid=(count +...]
    unnamed x15 -> x10, local copies, waits for them, and re-layouts: 3.51 us -> 0.03 us
    slice x1 -> x2, local copies, waits for them, and re-layouts: 0.01 us -> 2.73 us  [local(): gates = jnp.sum(jnp.where(match, routing[:, K:, None], 0.0), axis=1)]
    convert_element_type x0 -> x1, other arithmetic: none -> 2.61 us  [local(): pick = pick.astype(jnp.bfloat16)]
  transfers between devices with their start and end apart: 2 -> 2, of which waited for: 2 -> 2; matrix products, arithmetic and copies ran while one was open for 1% -> 4% of each run, Pallas kernels for 0% -> 0%
where the time goes in v3:
time: 247 us
  Pallas kernels  129 us (52%)
  waiting for transfers between devices  59.5 us (24%)
  blocking collectives  18.2 us (7%)
  between operations  13.6 us (6%)
  other arithmetic  10.1 us (4%)
  matrix products  9.76 us (4%)
  local copies, waits for them, and re-layouts  6.73 us (3%)
    pallas_call x1, Pallas kernels, run_experts(): pl.pallas_call(functools.partial(expert_kernel, n, count), grid=(count +...  87.5 us
    all_gather x1, waiting for transfers between devices, local(): moe_all = lax.all_gather(moe_rows, 'ctx', axis=0, tiled=True)  34.9 us
    pallas_call x1, Pallas kernels, gather_blocks(): pl.pallas_call(functools.partial(gather_kernel, n), out_shape=[jax.ShapeD...  28.2 us
    reduce_scatter x1, waiting for transfers between devices, local(): lax.psum_scatter(jnp.dot(attn_heads, w_out, preferred_element_type=jnp.fl...  24.5 us
    all_gather x1, blocking collectives, local(): lax.all_gather(post_cols, 'exp', axis=1, tiled=True).astype(jnp.float32)  18.2 us
    pallas_call x1, Pallas kernels, scatter_sum(): pl.pallas_call(functools.partial(scatter_kernel, n), out_shape=jax.ShapeD...  13.3 us
  transfers between devices with their start and end apart: 2, of which 2 were waited for; matrix products, arithmetic and copies ran while one was open for 4% of the time, Pallas kernels for 0%

profile of v3, /device:TPU:0, one launch (start us, length us, event | category | flops | bytes accessed | tf_op | source)
XLA Modules:
  0.0 246.8 jit_solution(13298108619789762299)
XLA Ops:
  6.5 0.8 convert_element_type.65
  7.4 0.7 pad_maximum_fusion
  8.1 0.7 copy.39.r_ref
  9.1 28.2 %shard_map.109 = (bf16[1536,512]{1,0:T(8,128)(2,1)}, bf16[1536,512]{1,0:T(8,128)(2,1)}, f32[1536,16]{1,0:T(8,128)}) custom-call(bf16[192,512]{1,0:T(8,128)(2,1)} %k_ref.1, bf16[192,512]{1,0:T(8,128)(2,1)} %v_ref.1, f32[192,16]{1,0:T(8,128)} %copy.39.r_ref), custom_call_target="tpu_custom_call" | custom-call | bytes 60000000 | tf_op jit(solution)/shard_map/pallas_call | solution.py:101
  37.3 2.5 %fusion.3 = (f32[192,4]{0,1:T(4,128)S(1)}, f32[4,1536,192]{1,2,0:T(8,128)S(1)}) fusion(pred[192,1536]{1,0:T(8,128)(4,1)S(1)} %iota_compare_fusion, bf16[1536,512]{1,0:T(8,128)(2,1)} %get-tuple-element.9, bf16[192,512]{1,0:T(8,128)(2,1)} %param.12), kind=kOutput, calls=%fused_computation.7 | convolution fusion | flops 305528064 | bytes 6786048 | tf_op jit(solution)/shard_map/qhd,khd->qhk/dot_general | solution.py:336
  39.9 1.5 fusion.6
  41.3 1.6 fusion.38
  42.9 1.5 convolution_convert_fusion
  44.5 24.5 %reduce-scatter.2.cloned.1.call-done = bf16[192,512]{1,0:T(8,128)(2,1)} async-done(((bf16[192,2048]{1,0:T(8,128)(2,1)}), bf16[192,512]{1,0:T(8,128)(2,1)}) %reduce-scatter.2.cloned.1.call-update) | async-done | bytes 196624 | tf_op jit(solution)/shard_map/reduce_scatter | solution.py:404
  69.0 1.0 add_convert_fusion.1
  70.0 18.2 %all_gather.6 = bf16[192,2048]{1,0:T(8,128)(2,1)S(1)} all-gather(bf16[192,512]{1,0:T(8,128)(2,1)S(1)} %add_convert_fusion.1), channel_id=1, replica_groups=mesh['ctx'=8,'exp'=4] {'exp'}, dimensions={1}, use_global_device_ids=true | all-gather | bytes 983040 | tf_op jit(solution)/shard_map/all_gather | solution.py:411
  88.2 0.2 fusion.13
  88.4 1.1 fusion.15
  89.6 1.4 fusion.62
  90.9 1.4 copy.49
  92.3 1.4 copy.44
  94.5 0.9 fusion.2
  95.3 1.6 reshape.99.g_ref
  97.0 2.6 %compare_convert_fusion.pick_ref = bf16[2,8,144,768]{3,2,1,0:T(8,128)(2,1)} fusion(f32[2,8,768]{2,1,0:T(8,128)S(1)} %copy.48, f32[144]{0:T(256)S(1)} %iota_convert_fusion), kind=kLoop, calls=%fused_computation.3 | loop fusion | flops 3538944 | bytes 3588672 | tf_op jit(solution)/shard_map/convert_element_type | solution.py:403
  99.6 34.9 %all-gather.2.cloned.1.call-done = bf16[1536,2048]{1,0:T(8,128)(2,1)} async-done(((bf16[192,2048]{1,0:T(8,128)(2,1)}), bf16[1536,2048]{1,0:T(8,128)(2,1)}) %all-gather.2.cloned.1.call-update) | async-done | bytes 6291472 | tf_op jit(solution)/shard_map/all_gather | solution.py:416
  134.5 87.5 %shard_map.110 = bf16[2,8,144,512]{3,2,1,0:T(8,128)(2,1)} custom-call(bf16[2,8,144,768]{3,2,1,0:T(8,128)(2,1)} %compare_convert_fusion.pick_ref, bf16[2,768,2048]{2,1,0:T(8,128)(2,1)} %bitcast.89, f32[8,288,1]{2,1,0:T(8,128)} %reshape.99.g_ref, bf16[8,2048,256]{2,1,0:T(8,128)(2,1)} %wg_ref.1, bf16[8,2048,256]{2,1,0:T(8,128)(2,1)} %wu_ref.1, ...), custom_call_target="tpu_custom_call" | custom-call | flops 8000000000 | bytes 100000000 | tf_op jit(solution)/shard_map/pallas_call | solution.py:230
  222.0 4.0 %bitcast_convert_fusion = bf16[2,768,512]{2,1,0:T(8,128)(2,1)S(1)} fusion(bf16[2,8,144,512]{3,2,1,0:T(8,128)(2,1)} %shard_map.110, f32[2,8,768]{2,1,0:T(8,128)S(1)} %copy.48, f32[144]{0:T(256)S(1)} %iota_convert_fusion), kind=kOutput, calls=%fused_computation.12 | convolution fusion | flops 1814495232 | bytes 3981888 | tf_op jit(solution)/shard_map/gjst,gjsd->gtd/dot_general | solution.py:427
  226.0 13.3 %shard_map.111 = f32[192,512]{1,0:T(8,128)S(1)} custom-call(bf16[8,192,512]{2,1,0:T(8,128)(2,1)S(1)} %bitcast.88), custom_call_target="tpu_custom_call" | custom-call | tf_op jit(solution)/shard_map/pallas_call | solution.py:314
  239.3 0.7 add_convert_fusion
  (30 shorter events, 1.1 us)
Async XLA Ops:
  6.5 36.4 %copy-start = (bf16[512,2048]{1,0:T(8,128)(2,1)S(1)}, bf16[512,2048]{1,0:T(8,128)(2,1)}, u32[]{:S(2)}) copy-start(bf16[512,2048]{1,0:T(8,128)(2,1)} %param.15) | copy-start | bytes 6291460
  6.5 62.5 %reduce-scatter.2.cloned.1.call-start = ((), (), s32[]{:S(2)}) async-start(), calls=%async_computation.1 | async-start | bytes 983040 | tf_op jit(solution)/shard_map/reduce_scatter | solution.py:404
  39.9 1.5 copy-start.4
  42.9 26.1 %copy-start.2 = (bf16[192,512]{1,0:T(8,128)(2,1)S(1)}, bf16[192,512]{1,0:T(8,128)(2,1)}, u32[]{:S(2)}) copy-start(bf16[192,512]{1,0:T(8,128)(2,1)} %param.11) | copy-start | bytes 589828
  42.9 45.5 %copy-start.3 = (f32[2048]{0:T(1024)S(1)}, f32[2048]{0:T(1024)}, u32[]{:S(2)}) copy-start(f32[2048]{0:T(1024)} %param.16) | copy-start | bytes 24580
  44.4 45.1 %copy-start.1 = (f32[1536,16]{1,0:T(8,128)S(1)}, f32[1536,16]{1,0:T(8,128)}, u32[]{:S(2)}) copy-start(f32[1536,16]{1,0:T(8,128)} %get-tuple-element.10) | copy-start | bytes 294916
  44.4 90.1 %all-gather.2.cloned.1.call-start = ((), (), s32[]{:S(2)}) async-start(), calls=%async_computation.2 | async-start | bytes 7077888 | tf_op jit(solution)/shard_map/all_gather | solution.py:416
Sparse Core Ops, SparseCore 0:
  44.5 24.4 reduce-scatter.1
  89.7 44.7 all-gather.1

commit v4 on v3

--- a/solution.py
+++ b/solution.py
@@ -323,6 +323,148 @@
     )(part)
 
 
+def norm_kernel(
+    n, part_ref, res_ref, gain_ref, rows_ref, post_ref, into, stage, wide, s_send, s_recv, send, recv
+):
+    me = lax.axis_index("exp")
+    width = res_ref.shape[1]
+    has_left, has_right = me > 0, me < n - 1
+    barrier = pltpu.get_barrier_semaphore()
+    for side, there in ((0, has_left), (1, has_right)):
+
+        @pl.when(there)
+        def _():
+            pl.semaphore_signal(
+                barrier,
+                inc=1,
+                device_id={"exp": me + 1 if side else me - 1},
+                device_id_type=MESH,
+            )
+
+    pl.semaphore_wait(barrier, jnp.minimum(me, 1) + jnp.minimum(n - 1 - me, 1))
+
+    def carry(side, target):
+        return pltpu.make_async_remote_copy(
+            src_ref=stage.at[target],
+            dst_ref=into.at[side, target],
+            send_sem=s_send.at[target],
+            recv_sem=s_recv.at[side, target],
+            device_id={"exp": me + 1 if side else me - 1},
+            device_id_type=MESH,
+        )
+
+    def hop(side, source):
+        return pltpu.make_async_remote_copy(
+            src_ref=wide.at[source],
+            dst_ref=wide.at[source],
+            send_sem=send.at[side, source],
+            recv_sem=recv.at[source],
+            device_id={"exp": me + 1 if side else me - 1},
+            device_id_type=MESH,
+        )
+
+    for i in range(n):
+        for side, target in ((1, n - 1 - i), (0, i)):
+            beyond = (target > me) if side else (target < me)
+            feeder = has_left if side else has_right
+            mine = part_ref.at[:, target * width : (target + 1) * width]
+
+            @pl.when(beyond & feeder)
+            def _():
+                carry(side, target).wait_recv()
+                total = mine[...].astype(jnp.float32) + into[side, target].astype(jnp.float32)
+                stage[target] = total.astype(jnp.bfloat16)
+
+            @pl.when(beyond & jnp.logical_not(feeder))
+            def _():
+                stage[target] = mine[...]
+
+            @pl.when(beyond)
+            def _():
+                carry(side, target).start()
+
+    for target in range(n):
+
+        @pl.when(target == me)
+        def _():
+            mine = part_ref[:, target * width : (target + 1) * width]
+            post_ref[...] = mine.astype(jnp.float32) + res_ref[...].astype(jnp.float32)
+            for side, feeder in ((1, has_left), (0, has_right)):
+
+                @pl.when(feeder)
+                def _():
+                    carry(side, target).wait_recv()
+                    post_ref[...] += into[side, target].astype(jnp.float32)
+
+    wide[me] = post_ref[...].astype(jnp.bfloat16)
+    for side, there in ((0, has_left), (1, has_right)):
+
+        @pl.when(there)
+        def _():
+            hop(side, me).start()
+
+    for distance in range(1, n):
+        for side in (0, 1):
+            source = me + distance if side == 0 else me - distance
+            onward = has_left if side == 0 else has_right
+            inside = (source < n) if side == 0 else (source >= 0)
+
+            @pl.when(inside)
+            def _():
+                hop(side, source).wait_recv()
+
+                @pl.when(onward)
+                def _():
+                    hop(side, source).start()
+
+    square_sum = jnp.zeros((res_ref.shape[0], 1), jnp.float32)
+    for source in range(n):
+        block = wide[source].astype(jnp.float32)
+        square_sum += jnp.sum(block * block, axis=1, keepdims=True)
+    scale = lax.rsqrt(square_sum / (n * width) + epsilon)
+    for source in range(n):
+        columns = slice(source * width, (source + 1) * width)
+        block = wide[source].astype(jnp.float32)
+        rows_ref[:, columns] = (block * scale * gain_ref[:, columns]).astype(jnp.bfloat16)
+    for index in range(n):
+        for side, there in ((0, has_left & (me <= index)), (1, has_right & (me >= index))):
+
+            @pl.when(there)
+            def _():
+                hop(side, index).wait_send()
+
+        for side, there in ((1, index > me), (0, index < me)):
+
+            @pl.when(there)
+            def _():
+                carry(side, index).wait_send()
+
+
+def sum_and_norm(part, residual, gain, n):
+    rows, width = residual.shape
+    return pl.pallas_call(
+        functools.partial(norm_kernel, n),
+        out_shape=(
+            jax.ShapeDtypeStruct((rows, n * width), jnp.bfloat16),
+            jax.ShapeDtypeStruct((rows, width), jnp.float32),
+        ),
+        in_specs=[pl.BlockSpec(memory_space=pltpu.VMEM)] * 3,
+        out_specs=[pl.BlockSpec(memory_space=pltpu.VMEM)] * 2,
+        scratch_shapes=[
+            pltpu.VMEM((2, n, rows, width), jnp.bfloat16),
+            pltpu.VMEM((n, rows, width), jnp.bfloat16),
+            pltpu.VMEM((n, rows, width), jnp.bfloat16),
+            pltpu.SemaphoreType.DMA((n,)),
+            pltpu.SemaphoreType.DMA((2, n)),
+            pltpu.SemaphoreType.DMA((2, n)),
+            pltpu.SemaphoreType.DMA((n,)),
+        ],
+        compiler_params=pltpu.CompilerParams(
+            collective_id=4, has_side_effects=True, vmem_limit_bytes=40 * 1024 * 1024
+        ),
+    )(part, residual, gain)
+
+
 def attend(carried, pieces, q_three, query_pos):
     row_max, row_total, row_accum = carried
     key_piece, value_piece = pieces
@@ -401,18 +543,13 @@
     gates_t = gates.reshape(groups, GROUP * block_rows, experts_here).transpose(0, 2, 1)
     slot_gate = jnp.sum(jnp.where(pick, gates_t[:, :, None, :], 0.0), axis=3)
     pick = pick.astype(jnp.bfloat16)
-    attn_cols = lax.psum_scatter(
+    moe_rows, post_sum = sum_and_norm(
         jnp.dot(attn_heads, w_out, preferred_element_type=jnp.float32).astype(jnp.bfloat16),
-        "exp",
-        scatter_dimension=1,
-        tiled=True,
-    ).astype(jnp.float32)
-    post_cols = (residual.astype(jnp.float32) + attn_cols).astype(jnp.bfloat16)
-    post_wide = lax.all_gather(post_cols, "exp", axis=1, tiled=True).astype(jnp.float32)
-    mean_square = jnp.mean(post_wide * post_wide, axis=1, keepdims=True)
-    moe_rows = (post_wide * lax.rsqrt(mean_square + epsilon) * moe_gain[None, :]).astype(
-        jnp.bfloat16
-    )
+        residual,
+        moe_gain[None, :],
+        lax.axis_size("exp"),
+    )
+    post_cols = post_sum.astype(jnp.bfloat16)
     moe_all = lax.all_gather(moe_rows, "ctx", axis=0, tiled=True)
     gate_column = slot_gate.transpose(1, 0, 2).reshape(experts_here, groups * GROUP * CAP, 1)
     expert_out = run_experts(

time: 247 us -> 244 us (0.988)
  Pallas kernels: 129 us -> 169 us
  waiting for transfers between devices: 59.5 us -> 37.6 us
  blocking collectives: 18.2 us -> 0 us
    pallas_call x0 -> x1, Pallas kernels: none -> 39.6 us  [sum_and_norm(): pl.pallas_call(functools.partial(norm_kernel, n), out_shape=(jax.ShapeDty...]
    reduce_scatter x1 -> x0, waiting for transfers between devices: 24.5 us -> none  [local(): lax.psum_scatter(jnp.dot(attn_heads, w_out, preferred_element_type=jnp.fl...]
    all_gather x1 -> x0, blocking collectives: 18.2 us -> none  [local(): lax.all_gather(post_cols, 'exp', axis=1, tiled=True).astype(jnp.float32)]
    all_gather x1, waiting for transfers between devices: 34.9 us -> 37.6 us  [local(): moe_all = lax.all_gather(moe_rows, 'ctx', axis=0, tiled=True)]
  transfers between devices with their start and end apart: 2 -> 1, of which waited for: 2 -> 1; matrix products, arithmetic and copies ran while one was open for 4% -> 4% of each run, Pallas kernels for 0% -> 0%
where the time goes in v4:
time: 244 us; the launch traced here: 243 us
  Pallas kernels  169 us (69%)
  waiting for transfers between devices  37.6 us (15%)
  between operations  13.6 us (6%)
  matrix products  8.99 us (4%)
  other arithmetic  7.74 us (3%)
  local copies, waits for them, and re-layouts  6.73 us (3%)
    pallas_call x1, Pallas kernels, run_experts(): pl.pallas_call(functools.partial(expert_kernel, n, count), grid=(count +...  87.5 us
    pallas_call x1, Pallas kernels, sum_and_norm(): pl.pallas_call(functools.partial(norm_kernel, n), out_shape=(jax.ShapeDty...  39.6 us
    all_gather x1, waiting for transfers between devices, local(): moe_all = lax.all_gather(moe_rows, 'ctx', axis=0, tiled=True)  37.6 us
    pallas_call x1, Pallas kernels, gather_blocks(): pl.pallas_call(functools.partial(gather_kernel, n), out_shape=[jax.ShapeD...  28.2 us
    pallas_call x1, Pallas kernels, scatter_sum(): pl.pallas_call(functools.partial(scatter_kernel, n), out_shape=jax.ShapeD...  13.3 us
  transfers between devices with their start and end apart: 1, of which 1 were waited for; matrix products, arithmetic and copies ran while one was open for 4% of the time, Pallas kernels for 0%

profile of v4, /device:TPU:0, one launch (start us, length us, event | category | flops | bytes accessed | tf_op | source)
XLA Modules:
  0.0 243.3 jit_solution(10243194682854711577)
XLA Ops:
  6.5 0.8 convert_element_type.52
  7.4 0.7 pad_maximum_fusion
  8.1 0.7 copy.39.r_ref
  8.8 0.2 iota_compare_fusion
  9.1 28.2 %shard_map.109 = (bf16[1536,512]{1,0:T(8,128)(2,1)}, bf16[1536,512]{1,0:T(8,128)(2,1)}, f32[1536,16]{1,0:T(8,128)}) custom-call(bf16[192,512]{1,0:T(8,128)(2,1)} %k_ref.1, bf16[192,512]{1,0:T(8,128)(2,1)} %v_ref.1, f32[192,16]{1,0:T(8,128)} %copy.39.r_ref), custom_call_target="tpu_custom_call" | custom-call | bytes 60000000 | tf_op jit(solution)/shard_map/pallas_call | solution.py:101
  37.3 2.7 %fusion.3 = (f32[192,4]{0,1:T(4,128)S(1)}, f32[4,1536,192]{1,2,0:T(8,128)S(1)}) fusion(pred[192,1536]{1,0:T(8,128)(4,1)S(1)} %iota_compare_fusion, bf16[1536,512]{1,0:T(8,128)(2,1)} %get-tuple-element.11, bf16[192,512]{1,0:T(8,128)(2,1)} %param.12), kind=kOutput, calls=%fused_computation.7 | convolution fusion | flops 305528064 | bytes 6786048 | tf_op jit(solution)/shard_map/qhd,khd->qhk/dot_general | solution.py:478
  40.0 1.5 fusion.6
  41.5 1.6 fusion.35
  43.1 0.6 convolution_convert_fusion.part_ref
  43.7 39.6 %shard_map.110 = (bf16[192,2048]{1,0:T(8,128)(2,1)}, f32[192,512]{1,0:T(8,128)S(1)}) custom-call(bf16[192,2048]{1,0:T(8,128)(2,1)S(1)} %convolution_convert_fusion.part_ref, bf16[192,512]{1,0:T(8,128)(2,1)S(1)} %copy-done.1, f32[1,2048]{1,0:T(1,128)S(1)} %bitcast.90), custom_call_target="tpu_custom_call" | custom-call | tf_op jit(solution)/shard_map/pallas_call | solution.py:445
  83.3 1.4 fusion.59
  84.7 1.4 copy.49
  86.0 1.4 copy.44
  87.4 0.1 compare_reduce_fusion
  87.7 0.2 fusion.24
  88.1 0.1 fusion.40
  88.2 0.9 fusion.2
  89.1 1.6 reshape.90.g_ref
  90.7 2.6 %compare_convert_fusion.pick_ref = bf16[2,8,144,768]{3,2,1,0:T(8,128)(2,1)} fusion(f32[2,8,768]{2,1,0:T(8,128)S(1)} %copy.48, f32[144]{0:T(256)S(1)} %iota_convert_fusion), kind=kLoop, calls=%fused_computation.3 | loop fusion | flops 3538944 | bytes 3588672 | tf_op jit(solution)/shard_map/convert_element_type | solution.py:545
  93.3 37.6 %all-gather.2.cloned.1.call-done = bf16[1536,2048]{1,0:T(8,128)(2,1)} async-done(((bf16[192,2048]{1,0:T(8,128)(2,1)}), bf16[1536,2048]{1,0:T(8,128)(2,1)}) %all-gather.2.cloned.1.call-update) | async-done | bytes 6291472 | tf_op jit(solution)/shard_map/all_gather | solution.py:553
  130.9 87.5 %shard_map.111 = bf16[2,8,144,512]{3,2,1,0:T(8,128)(2,1)} custom-call(bf16[2,8,144,768]{3,2,1,0:T(8,128)(2,1)} %compare_convert_fusion.pick_ref, bf16[2,768,2048]{2,1,0:T(8,128)(2,1)} %bitcast.91, f32[8,288,1]{2,1,0:T(8,128)} %reshape.90.g_ref, bf16[8,2048,256]{2,1,0:T(8,128)(2,1)} %wg_ref.1, bf16[8,2048,256]{2,1,0:T(8,128)(2,1)} %wu_ref.1, ...), custom_call_target="tpu_custom_call" | custom-call | flops 8000000000 | bytes 100000000 | tf_op jit(solution)/shard_map/pallas_call | solution.py:230
  218.4 4.0 %bitcast_convert_fusion = bf16[2,768,512]{2,1,0:T(8,128)(2,1)S(1)} fusion(bf16[2,8,144,512]{3,2,1,0:T(8,128)(2,1)} %shard_map.111, f32[2,8,768]{2,1,0:T(8,128)S(1)} %copy.48, f32[144]{0:T(256)S(1)} %iota_convert_fusion), kind=kOutput, calls=%fused_computation.12 | convolution fusion | flops 1814495232 | bytes 3981888 | tf_op jit(solution)/shard_map/gjst,gjsd->gtd/dot_general | solution.py:564
  222.4 13.3 %shard_map.112 = f32[192,512]{1,0:T(8,128)S(1)} custom-call(bf16[8,192,512]{2,1,0:T(8,128)(2,1)S(1)} %bitcast.89), custom_call_target="tpu_custom_call" | custom-call | tf_op jit(solution)/shard_map/pallas_call | solution.py:314
  235.7 0.7 add_convert_fusion
  (23 shorter events, 0.3 us)
Async XLA Ops:
  6.5 36.5 %copy-start = (bf16[512,2048]{1,0:T(8,128)(2,1)S(1)}, bf16[512,2048]{1,0:T(8,128)(2,1)}, u32[]{:S(2)}) copy-start(bf16[512,2048]{1,0:T(8,128)(2,1)} %param.15) | copy-start | bytes 6291460
  6.5 124.4 %all-gather.2.cloned.1.call-start = ((), (), s32[]{:S(2)}) async-start(), calls=%async_computation | async-start | bytes 7077888 | tf_op jit(solution)/shard_map/all_gather | solution.py:553
  37.3 4.2 %copy-start.4 = (bf16[1536,512]{1,0:T(8,128)(2,1)S(1)}, bf16[1536,512]{1,0:T(8,128)(2,1)}, u32[]{:S(2)}) copy-start(bf16[1536,512]{1,0:T(8,128)(2,1)} %get-tuple-element.10) | copy-start | bytes 4718596
  41.5 2.2 copy-start.1
  41.5 2.2 copy-start.2
  43.1 40.2 %copy-start.3 = (f32[1536,16]{1,0:T(8,128)S(1)}, f32[1536,16]{1,0:T(8,128)}, u32[]{:S(2)}) copy-start(f32[1536,16]{1,0:T(8,128)} %get-tuple-element.13) | copy-start | bytes 294916
Sparse Core Ops, SparseCore 0:
  83.4 47.4 all-gather.1
